TPU v7x, 128 devices: a whole 4x4x4 slice. The times are simulated.
128 devices in a mesh: band: 4 (over x_hi, core), dom: 32 (over z, y, x_lo).
Axes of the slice: x: 4 (x_hi: 2, x_lo: 2; x = x_hi * 2 + x_lo), y: 4, z: 4, core: 2. Of those that a mesh axis runs over, the one named last changes fastest.
Arguments:
- orbitals: float32 [128, 32, 48, 512], P('dom', None, None, 'band'), may hold values from -6 to 6
- potential: float32 [128, 32, 48], P('dom'), may hold values from -1 to 2
- projectors: float32 [256, 4, 4608], P('dom'), may hold values from -0.09375 to 0.09375
- coupling: float32 [256, 4, 4], P('dom'), may hold values from -4 to 4
- atom_plane: int32 [256], P('dom'), may hold values from 0 to 127, as said below
- projector_count: int32 [256], P('dom'), may hold values from 1 to 4
Outputs:
- filtered: float32 [128, 32, 48, 512], P('dom', None, None, 'band')
- gram: float32 [512, 512], replicated
Inputs may be any that keep to these rules, and one draw needn't show every extreme that they name: `atom_plane`: atom a's first plane lies among the 4 planes of dom index a // 8, that is from (a // 8) * 4 to (a // 8) * 4 + 3; the last atom of each dom index starts on that index's last plane.
All inputs are finite; a program needn't handle non-finite values.
Results may differ from a plain program's by a relative error of at most 0.0003.
Values sent between devices are 32-bit elements; how exact they have to be, the bound alone decides.
A program may use at most 192 MiB of HBM per device.

v0:
```python
import jax
import jax.numpy as jnp
from jax import lax
from jax.sharding import PartitionSpec as P

NORB = 512
HALO = 4
SPAN = 3
MAXPROJ = 4


center_weight = -205.0 / 72.0
side_weights = (8.0 / 5.0, -1.0 / 5.0, 8.0 / 315.0, -1.0 / 560.0)
HIGH = lax.Precision.HIGHEST


def with_halo(value, sides, width):
    for axis, dim in sides:
        peers, length = (lax.axis_size(axis), value.shape[dim])
        up = [(i, (i + 1) % peers) for i in range(peers)]
        down = [(j, i) for i, j in up]
        last = lax.slice_in_dim(value, length - width, length, axis=dim)
        first = lax.slice_in_dim(value, 0, width, axis=dim)
        before = lax.ppermute(last, axis, up)
        after = lax.ppermute(first, axis, down)
        value = jnp.concatenate([before, value, after], axis=dim)
    return value


def passed_along(value, axis, steps):
    count = lax.axis_size(axis)
    pairs = [(source, (source + steps) % count) for source in range(count)]
    return lax.ppermute(value, axis, pairs)


def laplacian(orbital_field, padded, planes):
    total = 3.0 * center_weight * orbital_field
    for offset in range(1, 5):
        weight = side_weights[offset - 1]
        total = total + weight * (
            padded[HALO + offset : HALO + offset + planes]
            + padded[HALO - offset : HALO - offset + planes]
        )
        total = total + weight * (
            jnp.roll(orbital_field, offset, 1) + jnp.roll(orbital_field, -offset, 1)
        )
        total = total + weight * (
            jnp.roll(orbital_field, offset, 2) + jnp.roll(orbital_field, -offset, 2)
        )
    return total


def apply_hamiltonian(orbital_field, potential, layout_pieces):
    planes, side_y, side_z, local_orbs = orbital_field.shape
    beta_full, live_mask, sym_coupling = layout_pieces
    padded = with_halo(orbital_field, (("dom", 0),), HALO)
    extended = padded[HALO : HALO + planes + SPAN - 1].reshape(
        planes + SPAN - 1, side_y * side_z, local_orbs
    )
    correlations = (
        jnp.einsum(
            "ajpc,pco->ajo", beta_full, extended, precision=HIGH, preferred_element_type=jnp.float32
        )
        * live_mask[:, :, None]
    )
    weighted = (
        jnp.einsum(
            "aij,ajo->aio",
            sym_coupling,
            correlations,
            precision=HIGH,
            preferred_element_type=jnp.float32,
        )
        * live_mask[:, :, None]
    )
    contrib = jnp.einsum(
        "ajpc,ajo->pco", beta_full, weighted, precision=HIGH, preferred_element_type=jnp.float32
    )
    contrib = contrib.reshape(planes + SPAN - 1, side_y, side_z, local_orbs)
    arrived = passed_along(contrib[planes:], "dom", 1)
    own_planes = contrib[:planes]
    own_planes = jnp.concatenate([own_planes[: SPAN - 1] + arrived, own_planes[SPAN - 1 :]], axis=0)
    kinetic = -0.5 * laplacian(orbital_field, padded, planes)
    return kinetic + potential[:, :, :, None] * orbital_field + own_planes


def shards(orbitals, potential, projectors, coupling, atom_plane, projector_count):
    planes, side_y, side_z, local_orbs = orbitals.shape
    atom_total = projectors.shape[0]
    first_plane = atom_plane - lax.axis_index("dom") * planes
    plane_ids = jnp.arange(planes + SPAN - 1, dtype=jnp.int32)
    span_ids = jnp.arange(SPAN, dtype=jnp.int32)
    onehot = (
        plane_ids[None, None, :] == first_plane[:, None, None] + span_ids[None, :, None]
    ).astype(jnp.float32)
    beta_split = projectors.reshape(atom_total, MAXPROJ, SPAN, side_y * side_z)
    beta_full = jnp.einsum(
        "akp,ajkc->ajpc", onehot, beta_split, precision=HIGH, preferred_element_type=jnp.float32
    )
    slots = jnp.arange(MAXPROJ, dtype=jnp.int32)
    live_mask = (slots[None, :] < projector_count[:, None]).astype(jnp.float32)
    sym_coupling = 0.5 * (coupling + jnp.transpose(coupling, (0, 2, 1)))
    layout_pieces = (beta_full, live_mask, sym_coupling)
    first = (apply_hamiltonian(orbitals, potential, layout_pieces) - 7.0 * orbitals) / 6.0
    second = (
        2.0 * (apply_hamiltonian(first, potential, layout_pieces) - 7.0 * first) / 6.0 - orbitals
    )
    cells = planes * side_y * side_z
    total_cells = cells * lax.axis_size("dom")
    flat = second.reshape(cells, local_orbs)
    identity = jnp.eye(NORB, dtype=jnp.float32)
    panels = lax.all_gather(flat, "band", axis=1, tiled=True)
    partial_gram = jnp.dot(panels.T, panels, precision=HIGH, preferred_element_type=jnp.float32)
    gram = lax.psum(partial_gram, "dom") * (1.0 / total_cells)
    lower = jnp.linalg.cholesky(gram)
    inverse = jax.scipy.linalg.solve_triangular(lower, identity, lower=True)
    own_rows = lax.dynamic_slice_in_dim(inverse, lax.axis_index("band") * local_orbs, local_orbs, 0)
    result = jnp.dot(panels, own_rows.T, precision=HIGH, preferred_element_type=jnp.float32)
    return (result.reshape(planes, side_y, side_z, local_orbs), gram)


def solution(mesh):
    placed = (
        P("dom", None, None, "band"),
        P("dom", None, None),
        P("dom", None, None),
        P("dom", None, None),
        P("dom"),
        P("dom"),
    )
    return jax.shard_map(
        shards,
        mesh=mesh,
        in_specs=placed,
        out_specs=(P("dom", None, None, "band"), P()),
        check_vma=False,
    )
```

profile of v0, /device:TPU:0, one launch (start us, length us, event | category | flops | bytes accessed | tf_op | source)
XLA Modules:
  0.0 1015.1 jit_solution(8115964120412169199)
XLA Ops:
  8.9 6.0 collective-permute-start
  43.0 41.0 %collective-permute-done.1 = f32[4,32,48,128]{3,2,1,0:T(8,128)} collective-permute-done((f32[4,32,48,128]{3,2,1,0:T(8,128)}, f32[4,32,48,128]{3,2,1,0:T(8,128)}, u32[]{:S(2)}, u32[]{:S(2)}) %collective-permute-start.1) | collective-permute-done | bytes 3145760 | tf_op jit(solution)/shard_map/ppermute | solution.py:24
  86.7 59.3 %collective-permute-done = f32[4,32,48,128]{3,2,1,0:T(8,128)} collective-permute-done((f32[4,32,48,128]{3,2,1,0:T(8,128)}, f32[4,32,48,128]{3,2,1,0:T(8,128)}, u32[]{:S(2)}, u32[]{:S(2)}) %collective-permute-start) | collective-permute-done | bytes 3145760 | tf_op jit(solution)/shard_map/ppermute | solution.py:25
  151.8 7.7 convolution_bitcast_fusion.1
  169.7 3.4 fusion.154
  173.1 27.3 %collective-permute-done.2 = f32[2,32,48,128]{3,2,1,0:T(8,128)S(1)} collective-permute-done((f32[2,32,48,128]{3,2,1,0:T(8,128)S(1)}, f32[2,32,48,128]{3,2,1,0:T(8,128)S(1)}, u32[]{:S(2)}, u32[]{:S(2)}) %collective-permute-start.2) | collective-permute-done | bytes 1572896 | tf_op jit(solution)/shard_map/ppermute | solution.py:33
  201.8 29.0 %broadcast_multiply_fusion = (f32[4,32,48,128]{3,2,1,0:T(8,128)S(1)}, f32[4,32,48,128]{3,2,1,0:T(8,128)}) fusion(f32[4,32,48,128]{3,2,1,0:T(8,128)S(1)} %copy-done, f32[2,32,48,128]{3,2,1,0:T(8,128)} %bitcast.108, f32[2,32,48,128]{3,2,1,0:T(8,128)} %add.258, f32[4,32,48]{2,1,0:T(8,128)} %param.7, f32[4,32,4,128]{3,2,1,0:T(4,128)} %get-tuple-element.95, ...), kind=kLoop, calls=%fused_computation.99 | loop fusion | flops 47972352 | bytes 88104960 | tf_op jit(solution)/shard_map/div | solution.py:104
  254.1 47.8 %collective-permute-done.3 = f32[4,32,48,128]{3,2,1,0:T(8,128)S(1)} collective-permute-done((f32[4,32,48,128]{3,2,1,0:T(8,128)S(1)}, f32[4,32,48,128]{3,2,1,0:T(8,128)S(1)}, u32[]{:S(2)}, u32[]{:S(2)}) %collective-permute-start.3) | collective-permute-done | bytes 3145760 | tf_op jit(solution)/shard_map/ppermute | solution.py:25
  305.7 8.0 convolution_bitcast_fusion
  324.4 77.6 %collective-permute-done.5 = f32[2,32,48,128]{3,2,1,0:T(8,128)S(1)} collective-permute-done((f32[2,32,48,128]{3,2,1,0:T(8,128)S(1)}, f32[2,32,48,128]{3,2,1,0:T(8,128)S(1)}, u32[]{:S(2)}, u32[]{:S(2)}) %collective-permute-start.5) | collective-permute-done | bytes 1572896 | tf_op jit(solution)/shard_map/ppermute | solution.py:33
  405.0 25.2 %multiply_subtract_fusion = f32[4,32,48,128]{3,2,1,0:T(8,128)} fusion(f32[4,32,48,128]{3,2,1,0:T(8,128)S(1)} %copy-done, f32[4,32,48,128]{3,2,1,0:T(8,128)S(1)} %copy-done.2, f32[2,32,48,128]{3,2,1,0:T(8,128)S(1)} %bitcast.109, f32[2,32,48,128]{3,2,1,0:T(8,128)} %add.285, f32[4,32,4,128]{3,2,1,0:T(4,128)} %get-tuple-element.61, ...), kind=kLoop, calls=%fused_computation.97 | loop fusion | flops 53477376 | bytes 72376320 | tf_op jit(solution)/shard_map/sub | solution.py:106
  430.3 85.4 %all-gather.2.cloned.1.call-done = f32[6144,512]{1,0:T(8,128)} async-done(((f32[6144,128]{1,0:T(8,128)}), f32[6144,512]{1,0:T(8,128)}) %all-gather.2.cloned.1.call-update) | async-done | bytes 12582928 | tf_op jit(solution)/shard_map/all_gather | solution.py:112
  515.6 26.2 %fusion.155 = f32[512,512]{0,1:T(8,128)} fusion(f32[6144,512]{1,0:T(8,128)} %all-gather.2.cloned.1.call-done), kind=kOutput, calls=%fused_computation.243 | convolution fusion | flops 19327352832 | bytes 13631488 | tf_op jit(solution)/shard_map/dot_general | solution.py:113
  543.8 307.9 %all-reduce.3.cloned.1.call-done = f32[512,512]{0,1:T(8,128)} async-done(((f32[512,512]{0,1:T(8,128)}), f32[512,512]{0,1:T(8,128)}) %all-reduce.3.cloned.1.call-update) | async-done | bytes 1048592 | tf_op jit(solution)/shard_map/psum | solution.py:114
  853.7 11.7 %cholesky.104 = f32[128,128]{1,0:T(8,128)S(1)} custom-call(f32[128,128]{1,0:T(8,128)S(1)} %cholesky.266), custom_call_target="Cholesky" | custom-call | tf_op jit(solution)/shard_map/jit(cholesky)/cholesky | solution.py:115
  865.6 9.8 custom-call.31
  877.1 11.7 %cholesky.217 = f32[128,128]{1,0:T(8,128)S(1)} custom-call(f32[128,128]{1,0:T(8,128)S(1)} %cholesky.270), custom_call_target="Cholesky" | custom-call | tf_op jit(solution)/shard_map/jit(cholesky)/cholesky | solution.py:115
  888.9 10.0 custom-call.32
  900.5 11.7 %cholesky.238 = f32[128,128]{1,0:T(8,128)S(1)} custom-call(f32[128,128]{1,0:T(8,128)S(1)} %cholesky.275), custom_call_target="Cholesky" | custom-call | tf_op jit(solution)/shard_map/jit(cholesky)/cholesky | solution.py:115
  912.9 9.8 custom-call.33
  924.1 11.9 %cholesky.255 = f32[128,128]{1,0:T(8,128)S(1)} custom-call(f32[128,128]{1,0:T(8,128)S(1)} %convolution_subtract_fusion.5), custom_call_target="Cholesky" | custom-call | tf_op jit(solution)/shard_map/jit(cholesky)/cholesky | solution.py:115
  940.0 10.1 while.1
  950.1 40.1 %custom-call.34 = f32[4,128,128]{1,2,0:T(8,128)S(1)} custom-call(f32[4,128,128]{2,1,0:T(8,128)} %get-tuple-element.9), custom_call_target="InvertDiagBlocksLowerTriangular" | custom-call | tf_op jit(solution)/shard_map/jit(_solve_triangular)/triangular_solve | solution.py:116
  994.1 13.8 %fusion.81 = f32[6144,128]{1,0:T(8,128)} fusion(f32[6144,512]{1,0:T(8,128)} %all-gather.2.cloned.1.call-done, s32[]{:T(128)S(6)} %select_n.8, f32[128,512]{1,0:T(8,128)S(1)} %fusion.84, f32[128,512]{1,0:T(8,128)S(1)} %fusion.96, f32[128,512]{1,0:T(8,128)S(1)} %fusion.94, f32[128,512]{1,0:T(8,128)S(1)} %fusion.93), kind=kOutput, calls=%fused_computation.138 | convolution fusion | flops 4832034816 | bytes 16777220 | tf_op jit(solution)/shard_map/dot_general | solution.py:118
  (135 shorter events, 115.3 us)
Async XLA Ops:
  7.2 13.9 %copy-start = (f32[4,32,48,128]{3,2,1,0:T(8,128)S(1)}, f32[4,32,48,128]{3,2,1,0:T(8,128)}, u32[]{:S(2)}) copy-start(f32[4,32,48,128]{3,2,1,0:T(8,128)} %param.6) | copy-start | bytes 9437188
  7.2 508.5 %all-gather.2.cloned.1.call-start = ((), (), s32[]{:S(2)}) async-start(), calls=%async_computation | async-start | bytes 15728640 | tf_op jit(solution)/shard_map/all_gather | solution.py:112
  7.2 76.8 %collective-permute-start.1 = (f32[4,32,48,128]{3,2,1,0:T(8,128)}, f32[4,32,48,128]{3,2,1,0:T(8,128)}, u32[]{:S(2)}, u32[]{:S(2)}) collective-permute-start(f32[4,32,48,128]{3,2,1,0:T(8,128)} %param.6), channel_id=1, source_target_pairs={{0,1},{1,2},{2,3},{3,4},{4,5},{5,6},{6,7},{7,8},{8,9},{9,10},{10,1... | collective-permute-start | bytes 9437192 | tf_op jit(solution)/shard_map/ppermute | solution.py:24
  8.9 137.1 %collective-permute-start = (f32[4,32,48,128]{3,2,1,0:T(8,128)}, f32[4,32,48,128]{3,2,1,0:T(8,128)}, u32[]{:S(2)}, u32[]{:S(2)}) collective-permute-start(f32[4,32,48,128]{3,2,1,0:T(8,128)} %param.6), channel_id=1, source_target_pairs={{1,0},{2,1},{3,2},{4,3},{5,4},{6,5},{7,6},{8,7},{9,8},{10,9},{11,1... | collective-permute-start | bytes 9437192 | tf_op jit(solution)/shard_map/ppermute | solution.py:25
  14.9 11.7 %copy-start.12 = (f32[8,4,4]{0,2,1:T(4,128)S(1)}, f32[8,4,4]{0,2,1:T(4,128)}, u32[]{:S(2)}) copy-start(f32[8,4,4]{0,2,1:T(4,128)} %param.9) | copy-start | bytes 1540
  14.9 11.8 %copy-start.13 = (s32[8]{0:T(128)S(1)}, s32[8]{0:T(128)}, u32[]{:S(2)}) copy-start(s32[8]{0:T(128)} %param.10) | copy-start | bytes 100
  30.4 121.3 %copy-start.3 = (f32[8,4,6,1536]{3,2,1,0:T(8,128)}, f32[8,4,6,1536]{3,2,1,0:T(8,128)S(1)}, u32[]{:S(2)}) copy-start(f32[8,4,6,1536]{3,2,1,0:T(8,128)S(1)} %convolution_bitcast_fusion.2) | copy-start | bytes 3538948
  86.7 64.9 %copy-start.1 = (f32[8,32,48,128]{3,2,1,0:T(8,128)}, f32[8,32,48,128]{3,2,1,0:T(8,128)S(1)}, u32[]{:S(2)}) copy-start(f32[8,32,48,128]{3,2,1,0:T(8,128)S(1)} %get-tuple-element.80) | copy-start | bytes 18874372
  159.5 2.9 copy-start.11
  160.9 39.5 %collective-permute-start.2 = (f32[2,32,48,128]{3,2,1,0:T(8,128)S(1)}, f32[2,32,48,128]{3,2,1,0:T(8,128)S(1)}, u32[]{:S(2)}, u32[]{:S(2)}) collective-permute-start(f32[2,32,48,128]{3,2,1,0:T(8,128)S(1)} %bitcast.112), channel_id=1, source_target_pairs={{0,1},{1,2},{2,3},{3,4},{4,5},{5,6},{6,7},{7,8},{8,9},{9,10},{10,1... | collective-permute-start | bytes 4718600 | tf_op jit(solution)/shard_map/ppermute | solution.py:33
  173.1 28.7 %copy-start.10 = (f32[4,1,48,128]{3,2,1,0:T(8,128)S(1)}, f32[4,1,48,128]{3,2,1,0:T(8,128)}, u32[]{:S(2)}) copy-start(f32[4,1,48,128]{3,2,1,0:T(8,128)} %get-tuple-element.64) | copy-start | bytes 294916
  230.8 71.1 %collective-permute-start.3 = (f32[4,32,48,128]{3,2,1,0:T(8,128)S(1)}, f32[4,32,48,128]{3,2,1,0:T(8,128)S(1)}, u32[]{:S(2)}, u32[]{:S(2)}) collective-permute-start(f32[4,32,48,128]{3,2,1,0:T(8,128)S(1)} %get-tuple-element.22), channel_id=1, source_target_pairs={{1,0},{2,1},{3,2},{4,3},{5,4},{6,5},{7,6},{8,7},{9,8},{10,9},{11,1... | collective-permute-start | bytes 9437192 | tf_op jit(solution)/shard_map/ppermute | solution.py:25
  234.3 169.0 %collective-permute-start.4 = (f32[4,32,48,128]{3,2,1,0:T(8,128)S(1)}, f32[4,32,48,128]{3,2,1,0:T(8,128)S(1)}, u32[]{:S(2)}, u32[]{:S(2)}) collective-permute-start(f32[4,32,48,128]{3,2,1,0:T(8,128)S(1)} %get-tuple-element.22), channel_id=1, source_target_pairs={{0,1},{1,2},{2,3},{3,4},{4,5},{5,6},{6,7},{7,8},{8,9},{9,10},{10,1... | collective-permute-start | bytes 9437192 | tf_op jit(solution)/shard_map/ppermute | solution.py:24
  254.1 48.4 %copy-start.4 = (f32[8,4,6,1536]{3,2,1,0:T(8,128)S(1)}, f32[8,4,6,1536]{3,2,1,0:T(8,128)}, u32[]{:S(2)}) copy-start(f32[8,4,6,1536]{3,2,1,0:T(8,128)} %copy-done.3) | copy-start | bytes 3538948
  314.0 88.0 %collective-permute-start.5 = (f32[2,32,48,128]{3,2,1,0:T(8,128)S(1)}, f32[2,32,48,128]{3,2,1,0:T(8,128)S(1)}, u32[]{:S(2)}, u32[]{:S(2)}) collective-permute-start(f32[2,32,48,128]{3,2,1,0:T(8,128)S(1)} %bitcast.111), channel_id=1, source_target_pairs={{0,1},{1,2},{2,3},{3,4},{4,5},{5,6},{6,7},{7,8},{8,9},{9,10},{10,1... | collective-permute-start | bytes 4718600 | tf_op jit(solution)/shard_map/ppermute | solution.py:33
  324.4 80.6 %copy-start.2 = (f32[4,32,48,128]{3,2,1,0:T(8,128)S(1)}, f32[4,32,48,128]{3,2,1,0:T(8,128)}, u32[]{:S(2)}) copy-start(f32[4,32,48,128]{3,2,1,0:T(8,128)} %get-tuple-element.23) | copy-start | bytes 9437188
  403.3 1.6 copy-start.8
  430.2 421.5 %all-reduce.3.cloned.1.call-start = ((), (), s32[]{:S(2)}) async-start(), calls=%async_computation.1 | async-start | bytes 2097152 | tf_op jit(solution)/shard_map/psum | solution.py:114
  851.7 1.8 copy-start.6
  853.4 45.7 %copy-start.5 = (f32[512,512]{1,0:T(8,128)}, f32[512,512]{1,0:T(8,128)S(1)}, u32[]{:S(2)}) copy-start(f32[512,512]{1,0:T(8,128)S(1)} %copy.20) | copy-start | bytes 3145732
  853.7 22.0 %copy-start.9 = (f32[512,512]{1,0:T(8,128)}, f32[512,512]{1,0:T(8,128)S(1)}, u32[]{:S(2)}) copy-start(f32[512,512]{1,0:T(8,128)S(1)} %fusion.64) | copy-start | bytes 3145732
  875.8 115.6 %copy-start.7 = (f32[512,512]{1,0:T(8,128)S(1)}, f32[512,512]{1,0:T(8,128)}, u32[]{:S(2)}) copy-start(f32[512,512]{1,0:T(8,128)} %fusion.77) | copy-start | bytes 3145732
Sparse Core Ops, SparseCore 0:
  430.3 85.2 all-gather.1
  542.0 309.6 all-reduce.2
where the time goes:
time: 1020 us
  waiting for transfers between devices  646 us (63%)
  other arithmetic  181 us (18%)
  local copies, waits for them, and re-layouts  85.5 us (8%)
  matrix products  72.9 us (7%)
  between operations  17.4 us (2%)
  starting transfers between devices  11.6 us (1%)
    psum x1, waiting for transfers between devices, shards(): gram = lax.psum(partial_gram, 'dom') * (1.0 / total_cells)  308 us
    ppermute x2, waiting for transfers between devices, with_halo(): after = lax.ppermute(first, axis, down)  107 us
    ppermute x2, waiting for transfers between devices, passed_along(): return lax.ppermute(value, axis, pairs)  105 us
    all_gather x1, waiting for transfers between devices, shards(): panels = lax.all_gather(flat, 'band', axis=1, tiled=True)  85.4 us
    another operation x14, other arithmetic, shards(): lower = jnp.linalg.cholesky(gram)  78.8 us
    ppermute x2, waiting for transfers between devices, with_halo(): before = lax.ppermute(last, axis, up)  41 us
    another operation x3, other arithmetic, shards(): inverse = jax.scipy.linalg.solve_triangular(lower, identity, lower=True)  40.3 us
    slice x16, local copies, waits for them, and re-layouts, laplacian(): jnp.roll(orbital_field, offset, 2) + jnp.roll(orbital_field, -offset, 2)  32.4 us
  transfers between devices with their start and end apart: 8, of which 7 were waited for; matrix products, arithmetic and copies ran while one was open for 9% of the time, Pallas kernels for 0%

commit v1 on v0

--- a/solution.py
+++ b/solution.py
@@ -1,6 +1,10 @@
+import functools
+
 import jax
 import jax.numpy as jnp
 from jax import lax
+from jax.experimental import pallas as pl
+from jax.experimental.pallas import tpu as pltpu
 from jax.sharding import PartitionSpec as P
 
 NORB = 512
@@ -12,6 +16,255 @@
 center_weight = -205.0 / 72.0
 side_weights = (8.0 / 5.0, -1.0 / 5.0, 8.0 / 315.0, -1.0 / 560.0)
 HIGH = lax.Precision.HIGHEST
+
+
+B = 128
+HIGHEST = lax.Precision.HIGHEST
+
+
+def dot_f32(a, b, dims):
+    return lax.dot_general(a, b, (dims, ((), ())), precision=HIGHEST, preferred_element_type=jnp.float32)
+
+
+def block_inverse(tiles):
+    count = len(tiles)
+    tiles = list(tiles)
+    shape = tiles[0].shape
+    lane = lax.broadcasted_iota(jnp.int32, shape, 1)
+    sub = lax.broadcasted_iota(jnp.int32, shape, 0)
+    done = []
+    for j in range(count):
+        base = 8 * j
+        cols = [
+            [jnp.broadcast_to(tiles[t][:, base + k : base + k + 1], shape) for k in range(8)]
+            for t in range(j, count)
+        ]
+        inside = (lane >= base) & (lane < base + 8)
+        unit = jnp.where(lane == sub + base, 1.0, 0.0)
+        own = jnp.where(inside, unit, tiles[j])
+        rows = [jnp.broadcast_to(own[k : k + 1, :], shape) for k in range(8)]
+        splat = [
+            [jnp.broadcast_to(cols[0][k][i : i + 1, :], shape) if i >= k else None for k in range(8)]
+            for i in range(8)
+        ]
+        rest = [jnp.where(inside, 0.0, tiles[t]) for t in range(j + 1, count)]
+        result = jnp.zeros(shape, jnp.float32)
+        for k in range(8):
+            scale = lax.rsqrt(splat[k][k])
+            rows[k] = rows[k] * scale
+            for i in range(k + 1, 8):
+                splat[i][k] = splat[i][k] * scale
+            for i in range(k + 1, 8):
+                for m in range(k + 1, i + 1):
+                    splat[i][m] = splat[i][m] - splat[i][k] * splat[m][k]
+                rows[i] = rows[i] - splat[i][k] * rows[k]
+            for t in range(len(rest)):
+                below = cols[t + 1]
+                below[k] = below[k] * scale
+                for m in range(k + 1, 8):
+                    below[m] = below[m] - below[k] * splat[m][k]
+                rest[t] = rest[t] - below[k] * rows[k]
+            result = jnp.where(sub == k, rows[k], result)
+        done.append(jnp.where(lane <= sub + base, result, 0.0))
+        tiles[j + 1 :] = rest
+    return done
+
+
+def factor_kernel(gram_ref, inverse_ref, work):
+    size = work.shape[0]
+    work[...] = gram_ref[...]
+
+    def step(k, carry):
+        at = pl.ds(pl.multiple_of(k * B, B), B)
+        tiles = [work[pl.ds(pl.multiple_of(k * B + 8 * t, 8), 8), at] for t in range(B // 8)]
+        corner = jnp.concatenate(block_inverse(tiles), axis=0)
+        row_id = lax.broadcasted_iota(jnp.int32, (size, B), 0)
+        column = jnp.where(row_id >= (k + 1) * B, work[:, at], 0.0)
+        unit = lax.broadcasted_iota(jnp.int32, (B, B), 0) == lax.broadcasted_iota(jnp.int32, (B, B), 1)
+        work[at, at] = jnp.where(unit, 1.0, 0.0)
+        below = dot_f32(column, corner, ((1,), (1,)))
+        scaled = dot_f32(corner, work[at, :], ((1,), (0,)))
+        block = work[:, at]
+        work[:, at] = jnp.where(row_id >= (k + 1) * B, 0.0, block)
+        work[...] = work[...] - dot_f32(below, scaled, ((1,), (0,)))
+        work[at, :] = scaled
+        return carry
+
+    lax.fori_loop(0, size // B, step, 0)
+    row_id = lax.broadcasted_iota(jnp.int32, (size, size), 0)
+    col_id = lax.broadcasted_iota(jnp.int32, (size, size), 1)
+    inverse_ref[...] = jnp.where(col_id <= row_id, work[...], 0.0)
+
+
+def inverse_factor(gram):
+    size = gram.shape[0]
+    return pl.pallas_call(
+        factor_kernel,
+        out_shape=jax.ShapeDtypeStruct((size, size), jnp.float32),
+        in_specs=[pl.BlockSpec(memory_space=pltpu.VMEM)],
+        out_specs=pl.BlockSpec(memory_space=pltpu.VMEM),
+        scratch_shapes=[pltpu.VMEM((size, size), jnp.float32)],
+        compiler_params=pltpu.CompilerParams(vmem_limit_bytes=32 * 2**20),
+    )(gram)
+
+
+MESH = pl.DeviceIdType.MESH
+B = 128
+NEAR = 8
+FAR = 16
+SUMMERS = 10
+
+
+def tri_blocks(size):
+    return [(i, j) for i in range(size // B) for j in range(i + 1)]
+
+
+def sum_kernel(factor, part_ref, gram_ref, pack, near, mine, far, total, near_s, near_r, far_s, far_r, out_s, out_r, end_s, end_r):
+    band, dom = lax.axis_index("band"), lax.axis_index("dom")
+    pair, half = dom // 2, dom % 2
+    rank = half * 4 + band
+    blocks = tri_blocks(part_ref.shape[0])
+    share = len(blocks) * B // NEAR
+    piece = share // SUMMERS
+
+    def near_peer(step):
+        other = (rank + step) % NEAR
+        return other, (other % 4, pair * 2 + other // 4)
+
+    def far_peer(step):
+        other = (pair + step) % FAR
+        return other, (band, other * 2 + half)
+
+    barrier = pltpu.get_barrier_semaphore()
+    for step in range(1, NEAR):
+        pl.semaphore_signal(barrier, inc=1, device_id=near_peer(step)[1], device_id_type=MESH)
+    for step in range(1, FAR):
+        pl.semaphore_signal(barrier, inc=1, device_id=far_peer(step)[1], device_id_type=MESH)
+    for n, (i, j) in enumerate(blocks):
+        pack[n * B : (n + 1) * B, :] = part_ref[i * B : (i + 1) * B, j * B : (j + 1) * B]
+    pl.semaphore_wait(barrier, NEAR + FAR - 2)
+
+    def rows(index, count):
+        return pl.ds(pl.multiple_of(index * count, 8), count)
+
+    def near_copy(step):
+        other, device = near_peer(step)
+        return pltpu.make_async_remote_copy(
+            src_ref=pack.at[rows(other, share)], dst_ref=near.at[rank],
+            send_sem=near_s.at[step], recv_sem=near_r.at[rank], device_id=device, device_id_type=MESH)
+
+    def near_arrival(step):
+        other, device = near_peer(step)
+        return pltpu.make_async_remote_copy(
+            src_ref=pack.at[rows(other, share)], dst_ref=near.at[other],
+            send_sem=near_s.at[step], recv_sem=near_r.at[other], device_id=device, device_id_type=MESH)
+
+    for step in range(1, NEAR):
+        near_copy(step).start()
+    near[rank] = pack[rows(rank, share), :]
+    for step in range(1, NEAR):
+        near_arrival(step).wait_recv()
+    acc = near[0]
+    for n in range(1, NEAR):
+        acc = acc + near[n]
+    mine[...] = acc
+
+    def far_copy(step, slot):
+        other, device = far_peer(step)
+        return other, pltpu.make_async_remote_copy(
+            src_ref=mine.at[rows(other % SUMMERS, piece)], dst_ref=far.at[pair if slot is None else other],
+            send_sem=far_s.at[step], recv_sem=far_r.at[pair if slot is None else other],
+            device_id=device, device_id_type=MESH)
+
+    for step in range(1, FAR):
+        other, copy = far_copy(step, None)
+        pl.when(other < SUMMERS)(copy.start)
+
+    place = rank * share
+
+    def out_rows(index):
+        return pl.ds(pl.multiple_of(place + (index % SUMMERS) * piece, 8), piece)
+
+    def out_copy(step):
+        other, device = far_peer(step)
+        return pltpu.make_async_remote_copy(
+            src_ref=total.at[out_rows(pair)], dst_ref=total.at[out_rows(pair)],
+            send_sem=out_s.at[step], recv_sem=out_r.at[pair], device_id=device, device_id_type=MESH)
+
+    def out_arrival(step):
+        other, device = far_peer(step)
+        return other, pltpu.make_async_remote_copy(
+            src_ref=total.at[out_rows(other)], dst_ref=total.at[out_rows(other)],
+            send_sem=out_s.at[step], recv_sem=out_r.at[other], device_id=device, device_id_type=MESH)
+
+    @pl.when(pair < SUMMERS)
+    def _():
+        far[pair] = mine[rows(pair % SUMMERS, piece), :]
+        for step in range(1, FAR):
+            far_copy(step, 1)[1].wait_recv()
+        acc = far[0]
+        for n in range(1, FAR):
+            acc = acc + far[n]
+        total[out_rows(pair), :] = acc * factor
+        for step in range(1, FAR):
+            out_copy(step).start()
+
+    for step in range(1, FAR):
+        other, copy = out_arrival(step)
+        pl.when(other < SUMMERS)(copy.wait_recv)
+
+    def end_copy(step, slot):
+        other, device = near_peer(step)
+        at = rows(rank if slot is None else other, share)
+        return pltpu.make_async_remote_copy(
+            src_ref=total.at[at], dst_ref=total.at[at],
+            send_sem=end_s.at[step], recv_sem=end_r.at[rank if slot is None else other],
+            device_id=device, device_id_type=MESH)
+
+    for step in range(1, NEAR):
+        end_copy(step, None).start()
+    for step in range(1, NEAR):
+        end_copy(step, 1).wait_recv()
+    for n, (i, j) in enumerate(blocks):
+        block = total[n * B : (n + 1) * B, :]
+        gram_ref[i * B : (i + 1) * B, j * B : (j + 1) * B] = block
+        if i != j:
+            gram_ref[j * B : (j + 1) * B, i * B : (i + 1) * B] = block.T
+
+    for step in range(1, NEAR):
+        near_copy(step).wait_send()
+        end_copy(step, None).wait_send()
+    for step in range(1, FAR):
+        other, copy = far_copy(step, None)
+        pl.when(other < SUMMERS)(copy.wait_send)
+
+    @pl.when(pair < SUMMERS)
+    def _():
+        for step in range(1, FAR):
+            out_copy(step).wait_send()
+
+
+def sum_gram(part, factor):
+    size = part.shape[0]
+    packed = len(tri_blocks(size)) * B
+    share = packed // NEAR
+    dma = pltpu.SemaphoreType.DMA
+    return pl.pallas_call(
+        functools.partial(sum_kernel, factor),
+        out_shape=jax.ShapeDtypeStruct((size, size), jnp.float32),
+        in_specs=[pl.BlockSpec(memory_space=pltpu.VMEM)],
+        out_specs=pl.BlockSpec(memory_space=pltpu.VMEM),
+        scratch_shapes=[
+            pltpu.VMEM((packed, B), jnp.float32),
+            pltpu.VMEM((NEAR, share, B), jnp.float32),
+            pltpu.VMEM((share, B), jnp.float32),
+            pltpu.VMEM((FAR, share // SUMMERS, B), jnp.float32),
+            pltpu.VMEM((packed, B), jnp.float32),
+            dma((NEAR,)), dma((NEAR,)), dma((FAR,)), dma((FAR,)),
+            dma((FAR,)), dma((FAR,)), dma((NEAR,)), dma((NEAR,)),
+        ],
+        compiler_params=pltpu.CompilerParams(collective_id=1, has_side_effects=True, vmem_limit_bytes=32 * 2**20),
+    )(part)
 
 
 def with_halo(value, sides, width):
@@ -108,12 +361,12 @@
     cells = planes * side_y * side_z
     total_cells = cells * lax.axis_size("dom")
     flat = second.reshape(cells, local_orbs)
-    identity = jnp.eye(NORB, dtype=jnp.float32)
     panels = lax.all_gather(flat, "band", axis=1, tiled=True)
-    partial_gram = jnp.dot(panels.T, panels, precision=HIGH, preferred_element_type=jnp.float32)
-    gram = lax.psum(partial_gram, "dom") * (1.0 / total_cells)
-    lower = jnp.linalg.cholesky(gram)
-    inverse = jax.scipy.linalg.solve_triangular(lower, identity, lower=True)
+    quarter = cells // lax.axis_size("band")
+    slab = lax.dynamic_slice_in_dim(panels, lax.axis_index("band") * quarter, quarter, 0)
+    partial_gram = jnp.dot(slab.T, slab, precision=HIGH, preferred_element_type=jnp.float32)
+    gram = sum_gram(partial_gram, 1.0 / total_cells)
+    inverse = inverse_factor(gram)
     own_rows = lax.dynamic_slice_in_dim(inverse, lax.axis_index("band") * local_orbs, local_orbs, 0)
     result = jnp.dot(panels, own_rows.T, precision=HIGH, preferred_element_type=jnp.float32)
     return (result.reshape(planes, side_y, side_z, local_orbs), gram)

time: 1020 us -> 613 us (0.60)
  waiting for transfers between devices: 646 us -> 340 us
  other arithmetic: 181 us -> 57.4 us
  Pallas kernels: 0 us -> 56.6 us
  matrix products: 72.9 us -> 46.1 us
  local copies, waits for them, and re-layouts: 85.5 us -> 75.3 us
    psum x1 -> x0, waiting for transfers between devices: 308 us -> none  [shards(): gram = lax.psum(partial_gram, 'dom') * (1.0 / total_cells)]
    another operation x17 -> x0, other arithmetic: 119 us -> none  [the longest x14 78.8 us: shards(): lower = jnp.linalg.cholesky(gram)]
    pallas_call x0 -> x2, Pallas kernels: none -> 56.6 us  [the longest x1 31.9 us: sum_gram(): pl.pallas_call(functools.partial(sum_kernel, factor), out_shape=jax.Shape...]
    dot_general x1, matrix products: 26.2 us -> 7.97 us  [shards(): jnp.dot(slab.T, slab, precision=HIGH, preferred_element_type=jnp.float32)]
    another operation x17 -> x0, local copies, waits for them, and re-layouts: 10.2 us -> none
  transfers between devices with their start and end apart: 8 -> 7, of which waited for: 7 -> 6; matrix products, arithmetic and copies ran while one was open for 9% -> 14% of each run, Pallas kernels for 0% -> 0%
where the time goes in v1:
time: 613 us; the launch traced here: 601 us
  waiting for transfers between devices  340 us (55%)
  local copies, waits for them, and re-layouts  75.3 us (12%)
  other arithmetic  57.4 us (9%)
  Pallas kernels  56.6 us (9%)
  matrix products  46.1 us (8%)
  between operations  14.4 us (2%)
  starting transfers between devices  11.5 us (2%)
    ppermute x2, waiting for transfers between devices, with_halo(): after = lax.ppermute(first, axis, down)  108 us
    ppermute x2, waiting for transfers between devices, passed_along(): return lax.ppermute(value, axis, pairs)  104 us
    all_gather x1, waiting for transfers between devices, shards(): panels = lax.all_gather(flat, 'band', axis=1, tiled=True)  85.4 us
    ppermute x2, waiting for transfers between devices, with_halo(): before = lax.ppermute(last, axis, up)  41.8 us
    pallas_call x1, Pallas kernels, sum_gram(): pl.pallas_call(functools.partial(sum_kernel, factor), out_shape=jax.Shape...  31.9 us
    slice x16, local copies, waits for them, and re-layouts, laplacian(): jnp.roll(orbital_field, offset, 1) + jnp.roll(orbital_field, -offset, 1)  31.1 us
    slice x16, local copies, waits for them, and re-layouts, laplacian(): jnp.roll(orbital_field, offset, 2) + jnp.roll(orbital_field, -offset, 2)  31 us
    div x1, other arithmetic, shards(): (apply_hamiltonian(orbitals, potential, layout_pieces) - 7.0 * orbitals)...  28.9 us
  transfers between devices with their start and end apart: 7, of which 6 were waited for; matrix products, arithmetic and copies ran while one was open for 14% of the time, Pallas kernels for 0%

profile of v1, /device:TPU:0, one launch (start us, length us, event | category | flops | bytes accessed | tf_op | source)
XLA Modules:
  0.0 601.3 jit_solution(11045979627059735965)
XLA Ops:
  8.9 6.0 collective-permute-start
  38.7 3.1 fusion.107
  42.3 41.7 %collective-permute-done.1 = f32[4,32,48,128]{3,2,1,0:T(8,128)} collective-permute-done((f32[4,32,48,128]{3,2,1,0:T(8,128)}, f32[4,32,48,128]{3,2,1,0:T(8,128)}, u32[]{:S(2)}, u32[]{:S(2)}) %collective-permute-start.1) | collective-permute-done | bytes 3145760 | tf_op jit(solution)/shard_map/ppermute | solution.py:277
  86.7 59.3 %collective-permute-done = f32[4,32,48,128]{3,2,1,0:T(8,128)} collective-permute-done((f32[4,32,48,128]{3,2,1,0:T(8,128)}, f32[4,32,48,128]{3,2,1,0:T(8,128)}, u32[]{:S(2)}, u32[]{:S(2)}) %collective-permute-start) | collective-permute-done | bytes 3145760 | tf_op jit(solution)/shard_map/ppermute | solution.py:278
  148.4 3.2 fusion.65
  151.8 7.7 %convolution_bitcast_fusion.1 = f32[6,1536,128]{2,1,0:T(8,128)S(1)} fusion(f32[8,4,6,1536]{3,2,1,0:T(8,128)S(1)} %convolution_bitcast_fusion.2, f32[8,4,128]{2,1,0:T(4,128)S(1)} %fusion.76, f32[8,4]{0,1:T(4,128)S(1)} %fusion.84), kind=kOutput, calls=%fused_computation.12 | convolution fusion | flops 452988928 | bytes 5914752 | tf_op jit(solution)/shard_map/ajpc,ajo->pco/dot_general | solution.py:329
  163.1 3.2 fusion.113
  166.3 3.2 fusion.117
  169.5 3.2 fusion.121
  172.7 27.7 %collective-permute-done.2 = f32[2,32,48,128]{3,2,1,0:T(8,128)S(1)} collective-permute-done((f32[2,32,48,128]{3,2,1,0:T(8,128)S(1)}, f32[2,32,48,128]{3,2,1,0:T(8,128)S(1)}, u32[]{:S(2)}, u32[]{:S(2)}) %collective-permute-start.2) | collective-permute-done | bytes 1572896 | tf_op jit(solution)/shard_map/ppermute | solution.py:286
  201.8 28.9 %broadcast_multiply_fusion = (f32[4,32,48,128]{3,2,1,0:T(8,128)S(1)}, f32[4,32,48,128]{3,2,1,0:T(8,128)}) fusion(f32[4,32,48,128]{3,2,1,0:T(8,128)S(1)} %copy-done, f32[2,32,48,128]{3,2,1,0:T(8,128)} %bitcast.58, f32[2,32,48,128]{3,2,1,0:T(8,128)} %add.218, f32[4,32,48]{2,1,0:T(8,128)} %param.7, f32[4,32,4,128]{3,2,1,0:T(4,128)} %get-tuple-element.73, ...), kind=kLoop, calls=%fused_computation.99 | loop fusion | flops 47972352 | bytes 88104960 | tf_op jit(solution)/shard_map/div | solution.py:357
  252.7 49.2 %collective-permute-done.3 = f32[4,32,48,128]{3,2,1,0:T(8,128)S(1)} collective-permute-done((f32[4,32,48,128]{3,2,1,0:T(8,128)S(1)}, f32[4,32,48,128]{3,2,1,0:T(8,128)S(1)}, u32[]{:S(2)}, u32[]{:S(2)}) %collective-permute-start.3) | collective-permute-done | bytes 3145760 | tf_op jit(solution)/shard_map/ppermute | solution.py:278
  302.1 3.2 fusion.64
  305.5 7.9 %convolution_bitcast_fusion = f32[6,1536,128]{2,1,0:T(8,128)S(1)} fusion(f32[8,4,6,1536]{3,2,1,0:T(8,128)S(1)} %copy-done.4, f32[8,4,128]{2,1,0:T(4,128)S(1)} %fusion.74, f32[8,4]{0,1:T(4,128)S(1)} %fusion.84), kind=kOutput, calls=%fused_computation.11 | convolution fusion | flops 452988928 | bytes 5914752 | tf_op jit(solution)/shard_map/ajpc,ajo->pco/dot_general | solution.py:329
  315.6 3.2 fusion.97
  318.8 3.1 fusion.101
  321.9 3.2 fusion.105
  325.2 76.8 %collective-permute-done.5 = f32[2,32,48,128]{3,2,1,0:T(8,128)S(1)} collective-permute-done((f32[2,32,48,128]{3,2,1,0:T(8,128)S(1)}, f32[2,32,48,128]{3,2,1,0:T(8,128)S(1)}, u32[]{:S(2)}, u32[]{:S(2)}) %collective-permute-start.5) | collective-permute-done | bytes 1572896 | tf_op jit(solution)/shard_map/ppermute | solution.py:286
  405.0 24.7 %multiply_subtract_fusion = f32[4,32,48,128]{3,2,1,0:T(8,128)} fusion(f32[4,32,48,128]{3,2,1,0:T(8,128)S(1)} %copy-done, f32[4,32,48,128]{3,2,1,0:T(8,128)S(1)} %copy-done.2, f32[2,32,48,128]{3,2,1,0:T(8,128)} %bitcast.59, f32[2,32,48,128]{3,2,1,0:T(8,128)} %add.245, f32[4,32,4,128]{3,2,1,0:T(4,128)} %get-tuple-element.39, ...), kind=kLoop, calls=%fused_computation.97 | loop fusion | flops 53477376 | bytes 72376320 | tf_op jit(solution)/shard_map/sub | solution.py:359
  429.8 85.4 %all-gather.2.cloned.1.call-done = f32[6144,512]{1,0:T(8,128)} async-done(((f32[6144,128]{1,0:T(8,128)}), f32[6144,512]{1,0:T(8,128)}) %all-gather.2.cloned.1.call-update) | async-done | bytes 12582928 | tf_op jit(solution)/shard_map/all_gather | solution.py:364
  515.2 8.0 %fusion.62.part_ref = f32[512,512]{1,0:T(8,128)S(1)} fusion(f32[6144,512]{1,0:T(8,128)} %all-gather.2.cloned.1.call-done, s32[]{:T(128)S(6)} %select_n.6), kind=kOutput, calls=%fused_computation.95 | convolution fusion | flops 4831838208 | bytes 4194308 | tf_op jit(solution)/shard_map/dot_general | solution.py:367
  523.2 31.9 %shard_map.77.gram_ref = f32[512,512]{1,0:T(8,128)S(1)} custom-call(f32[512,512]{1,0:T(8,128)S(1)} %fusion.62.part_ref), custom_call_target="tpu_custom_call" | custom-call | tf_op jit(solution)/shard_map/pallas_call | solution.py:252
  555.1 24.6 %shard_map.78 = f32[512,512]{1,0:T(8,128)S(1)} custom-call(f32[512,512]{1,0:T(8,128)S(1)} %shard_map.77.gram_ref), custom_call_target="tpu_custom_call" | custom-call | tf_op jit(solution)/shard_map/pallas_call | solution.py:101
  579.7 13.5 %fusion.70 = f32[6144,128]{1,0:T(8,128)} fusion(f32[6144,512]{1,0:T(8,128)} %all-gather.2.cloned.1.call-done, f32[512,512]{1,0:T(8,128)S(1)} %shard_map.78, s32[]{:T(128)S(6)} %select_n.7), kind=kOutput, calls=%fused_computation.108 | convolution fusion | flops 4831838208 | bytes 15990788 | tf_op jit(solution)/shard_map/dot_general | solution.py:371
  (73 shorter events, 64.7 us)
Async XLA Ops:
  7.2 13.9 %copy-start = (f32[4,32,48,128]{3,2,1,0:T(8,128)S(1)}, f32[4,32,48,128]{3,2,1,0:T(8,128)}, u32[]{:S(2)}) copy-start(f32[4,32,48,128]{3,2,1,0:T(8,128)} %param.6) | copy-start | bytes 9437188
  7.2 508.0 %all-gather.2.cloned.1.call-start = ((), (), s32[]{:S(2)}) async-start(), calls=%async_computation | async-start | bytes 15728640 | tf_op jit(solution)/shard_map/all_gather | solution.py:364
  7.2 76.8 %collective-permute-start.1 = (f32[4,32,48,128]{3,2,1,0:T(8,128)}, f32[4,32,48,128]{3,2,1,0:T(8,128)}, u32[]{:S(2)}, u32[]{:S(2)}) collective-permute-start(f32[4,32,48,128]{3,2,1,0:T(8,128)} %param.6), channel_id=1, source_target_pairs={{0,1},{1,2},{2,3},{3,4},{4,5},{5,6},{6,7},{7,8},{8,9},{9,10},{10,1... | collective-permute-start | bytes 9437192 | tf_op jit(solution)/shard_map/ppermute | solution.py:277
  8.9 137.1 %collective-permute-start = (f32[4,32,48,128]{3,2,1,0:T(8,128)}, f32[4,32,48,128]{3,2,1,0:T(8,128)}, u32[]{:S(2)}, u32[]{:S(2)}) collective-permute-start(f32[4,32,48,128]{3,2,1,0:T(8,128)} %param.6), channel_id=1, source_target_pairs={{1,0},{2,1},{3,2},{4,3},{5,4},{6,5},{7,6},{8,7},{9,8},{10,9},{11,1... | collective-permute-start | bytes 9437192 | tf_op jit(solution)/shard_map/ppermute | solution.py:278
  14.9 11.6 %copy-start.7 = (f32[8,4,4]{0,2,1:T(4,128)S(1)}, f32[8,4,4]{0,2,1:T(4,128)}, u32[]{:S(2)}) copy-start(f32[8,4,4]{0,2,1:T(4,128)} %param.9) | copy-start | bytes 1540
  14.9 11.7 %copy-start.9 = (s32[8]{0:T(128)S(1)}, s32[8]{0:T(128)}, u32[]{:S(2)}) copy-start(s32[8]{0:T(128)} %param.10) | copy-start | bytes 100
  18.9 8.6 %copy-start.8 = (s32[8]{0:T(128)S(1)}, s32[8]{0:T(128)}, u32[]{:S(2)}) copy-start(s32[8]{0:T(128)} %param.11) | copy-start | bytes 100
  29.8 122.0 %copy-start.3 = (f32[8,4,6,1536]{3,2,1,0:T(8,128)}, f32[8,4,6,1536]{3,2,1,0:T(8,128)S(1)}, u32[]{:S(2)}) copy-start(f32[8,4,6,1536]{3,2,1,0:T(8,128)S(1)} %convolution_bitcast_fusion.2) | copy-start | bytes 3538948
  86.7 61.4 %copy-start.1 = (f32[8,32,48,128]{3,2,1,0:T(8,128)}, f32[8,32,48,128]{3,2,1,0:T(8,128)S(1)}, u32[]{:S(2)}) copy-start(f32[8,32,48,128]{3,2,1,0:T(8,128)S(1)} %get-tuple-element.58) | copy-start | bytes 18874372
  159.5 2.9 copy-start.6
  160.9 39.5 %collective-permute-start.2 = (f32[2,32,48,128]{3,2,1,0:T(8,128)S(1)}, f32[2,32,48,128]{3,2,1,0:T(8,128)S(1)}, u32[]{:S(2)}, u32[]{:S(2)}) collective-permute-start(f32[2,32,48,128]{3,2,1,0:T(8,128)S(1)} %bitcast.62), channel_id=1, source_target_pairs={{0,1},{1,2},{2,3},{3,4},{4,5},{5,6},{6,7},{7,8},{8,9},{9,10},{10,1... | collective-permute-start | bytes 4718600 | tf_op jit(solution)/shard_map/ppermute | solution.py:286
  230.7 71.1 %collective-permute-start.3 = (f32[4,32,48,128]{3,2,1,0:T(8,128)S(1)}, f32[4,32,48,128]{3,2,1,0:T(8,128)S(1)}, u32[]{:S(2)}, u32[]{:S(2)}) collective-permute-start(f32[4,32,48,128]{3,2,1,0:T(8,128)S(1)} %get-tuple-element.2), channel_id=1, source_target_pairs={{1,0},{2,1},{3,2},{4,3},{5,4},{6,5},{7,6},{8,7},{9,8},{10,9},{11,1... | collective-permute-start | bytes 9437192 | tf_op jit(solution)/shard_map/ppermute | solution.py:278
  234.3 169.0 %collective-permute-start.4 = (f32[4,32,48,128]{3,2,1,0:T(8,128)S(1)}, f32[4,32,48,128]{3,2,1,0:T(8,128)S(1)}, u32[]{:S(2)}, u32[]{:S(2)}) collective-permute-start(f32[4,32,48,128]{3,2,1,0:T(8,128)S(1)} %get-tuple-element.2), channel_id=1, source_target_pairs={{0,1},{1,2},{2,3},{3,4},{4,5},{5,6},{6,7},{7,8},{8,9},{9,10},{10,1... | collective-permute-start | bytes 9437192 | tf_op jit(solution)/shard_map/ppermute | solution.py:277
  252.7 49.5 %copy-start.4 = (f32[8,4,6,1536]{3,2,1,0:T(8,128)S(1)}, f32[8,4,6,1536]{3,2,1,0:T(8,128)}, u32[]{:S(2)}) copy-start(f32[8,4,6,1536]{3,2,1,0:T(8,128)} %copy-done.3) | copy-start | bytes 3538948
  314.9 87.0 %collective-permute-start.5 = (f32[2,32,48,128]{3,2,1,0:T(8,128)S(1)}, f32[2,32,48,128]{3,2,1,0:T(8,128)S(1)}, u32[]{:S(2)}, u32[]{:S(2)}) collective-permute-start(f32[2,32,48,128]{3,2,1,0:T(8,128)S(1)} %bitcast.61), channel_id=1, source_target_pairs={{0,1},{1,2},{2,3},{3,4},{4,5},{5,6},{6,7},{7,8},{8,9},{9,10},{10,1... | collective-permute-start | bytes 4718600 | tf_op jit(solution)/shard_map/ppermute | solution.py:286
  325.2 79.9 %copy-start.2 = (f32[4,32,48,128]{3,2,1,0:T(8,128)S(1)}, f32[4,32,48,128]{3,2,1,0:T(8,128)}, u32[]{:S(2)}) copy-start(f32[4,32,48,128]{3,2,1,0:T(8,128)} %get-tuple-element.3) | copy-start | bytes 9437188
  403.3 1.7 copy-start.5
Sparse Core Ops, SparseCore 0:
  429.9 85.2 all-gather.1

commit v2 on v1

--- a/solution.py
+++ b/solution.py
@@ -11,14 +11,13 @@
 HALO = 4
 SPAN = 3
 MAXPROJ = 4
-
+B = 128
 
 center_weight = -205.0 / 72.0
 side_weights = (8.0 / 5.0, -1.0 / 5.0, 8.0 / 315.0, -1.0 / 560.0)
 HIGH = lax.Precision.HIGHEST
 
 
-B = 128
 HIGHEST = lax.Precision.HIGHEST
 
 
@@ -109,7 +108,6 @@
 
 
 MESH = pl.DeviceIdType.MESH
-B = 128
 NEAR = 8
 FAR = 16
 SUMMERS = 10
@@ -267,109 +265,430 @@
     )(part)
 
 
-def with_halo(value, sides, width):
-    for axis, dim in sides:
-        peers, length = (lax.axis_size(axis), value.shape[dim])
-        up = [(i, (i + 1) % peers) for i in range(peers)]
-        down = [(j, i) for i, j in up]
-        last = lax.slice_in_dim(value, length - width, length, axis=dim)
-        first = lax.slice_in_dim(value, 0, width, axis=dim)
-        before = lax.ppermute(last, axis, up)
-        after = lax.ppermute(first, axis, down)
-        value = jnp.concatenate([before, value, after], axis=dim)
-    return value
-
-
-def passed_along(value, axis, steps):
-    count = lax.axis_size(axis)
-    pairs = [(source, (source + steps) % count) for source in range(count)]
-    return lax.ppermute(value, axis, pairs)
-
-
-def laplacian(orbital_field, padded, planes):
-    total = 3.0 * center_weight * orbital_field
-    for offset in range(1, 5):
-        weight = side_weights[offset - 1]
-        total = total + weight * (
-            padded[HALO + offset : HALO + offset + planes]
-            + padded[HALO - offset : HALO - offset + planes]
-        )
-        total = total + weight * (
-            jnp.roll(orbital_field, offset, 1) + jnp.roll(orbital_field, -offset, 1)
-        )
-        total = total + weight * (
-            jnp.roll(orbital_field, offset, 2) + jnp.roll(orbital_field, -offset, 2)
-        )
-    return total
-
-
-def apply_hamiltonian(orbital_field, potential, layout_pieces):
-    planes, side_y, side_z, local_orbs = orbital_field.shape
-    beta_full, live_mask, sym_coupling = layout_pieces
-    padded = with_halo(orbital_field, (("dom", 0),), HALO)
-    extended = padded[HALO : HALO + planes + SPAN - 1].reshape(
-        planes + SPAN - 1, side_y * side_z, local_orbs
-    )
-    correlations = (
-        jnp.einsum(
-            "ajpc,pco->ajo", beta_full, extended, precision=HIGH, preferred_element_type=jnp.float32
-        )
-        * live_mask[:, :, None]
-    )
-    weighted = (
-        jnp.einsum(
-            "aij,ajo->aio",
-            sym_coupling,
-            correlations,
-            precision=HIGH,
-            preferred_element_type=jnp.float32,
-        )
-        * live_mask[:, :, None]
-    )
-    contrib = jnp.einsum(
-        "ajpc,ajo->pco", beta_full, weighted, precision=HIGH, preferred_element_type=jnp.float32
-    )
-    contrib = contrib.reshape(planes + SPAN - 1, side_y, side_z, local_orbs)
-    arrived = passed_along(contrib[planes:], "dom", 1)
-    own_planes = contrib[:planes]
-    own_planes = jnp.concatenate([own_planes[: SPAN - 1] + arrived, own_planes[SPAN - 1 :]], axis=0)
-    kinetic = -0.5 * laplacian(orbital_field, padded, planes)
-    return kinetic + potential[:, :, :, None] * orbital_field + own_planes
+PLANES = 8
+ROWS = 16
+DEPTH = 48
+CELLS = ROWS * DEPTH
+PROJ = 32
+REACH = 6
+FLAGS = PROJ
+
+
+def shift_terms(field, p, r):
+    centre = field[p + HALO, r + HALO]
+    terms = []
+    for k in range(1, 5):
+        pair_x = field[p + HALO + k, r + HALO] + field[p + HALO - k, r + HALO]
+        pair_y = field[p + HALO, r + HALO + k] + field[p + HALO, r + HALO - k]
+        pair_z = pltpu.roll(centre, k, 0) + pltpu.roll(centre, DEPTH - k, 0)
+        terms.append((pair_x + pair_y) + pair_z)
+    return centre, terms
+
+
+def split(value):
+    high = value.astype(jnp.bfloat16)
+    return high, (value - high.astype(jnp.float32)).astype(jnp.bfloat16)
+
+
+def plane_order(i):
+    return lax.rem(i, 2) * 4 + i // 2
+
+
+def field_kernel(
+    orb, pot, proj, info, slab,
+    e1, e2, second, shift_pot, nonlocal_plane, left, right, raw, notes, pot_all, corr, corr_in, weights,
+    local_s, x_s, x_r, own_s, fwd_s, halo_r, edge_s, edge_r, small_s, small_r, next_s, next_r,
+    corr_s, corr_r, y2_s, y2_r, edge2_s, edge2_r, out_s, out_r,
+):
+    band, dom = lax.axis_index("band"), lax.axis_index("dom")
+    pair, half = dom // 2, dom % 2
+    other = 1 - half
+    pairs = lax.axis_size("dom") // 2
+    partner = (band, pair * 2 + other)
+
+    def at_pair(step):
+        return (band, lax.rem(pair + step + pairs, pairs) * 2 + half)
+
+    def send(src, dst, ssem, rsem, device):
+        return pltpu.make_async_remote_copy(
+            src_ref=src, dst_ref=dst, send_sem=ssem, recv_sem=rsem, device_id=device, device_id_type=MESH)
+
+    barrier = pltpu.get_barrier_semaphore()
+    for peer in [at_pair(1), at_pair(-1)] + [(b, pair * 2 + other) for b in range(4)]:
+        pl.semaphore_signal(barrier, inc=1, device_id=peer, device_id_type=MESH)
+
+    def rows_of(which):
+        return pl.ds(pl.multiple_of(which * ROWS, 8), ROWS)
+
+    own_planes = pl.ds(HALO + 4 * half, 4)
+    main = pl.ds(HALO, ROWS)
+
+    def edge_rows(which, side):
+        return pl.ds(pl.multiple_of(lax.rem(which * ROWS + (28 if side == 0 else 16), 32), 4), 4)
+
+    low, high = pl.ds(0, 4), pl.ds(HALO + ROWS, 4)
+    locals_ = [
+        pltpu.make_async_copy(orb.at[:, rows_of(half)], e1.at[own_planes, main], local_s.at[0]),
+        pltpu.make_async_copy(orb.at[:, edge_rows(half, 0)], e1.at[own_planes, low], local_s.at[1]),
+        pltpu.make_async_copy(orb.at[:, edge_rows(half, 1)], e1.at[own_planes, high], local_s.at[2]),
+    ]
+    for copy in locals_:
+        copy.start()
+
+    small = [
+        send(pot.at[:, rows_of(other)], pot_all.at[pl.ds(4 * half, 4)], small_s.at[0], small_r.at[0], partner),
+        send(info, notes.at[1 + half], small_s.at[1], small_r.at[1], partner),
+        send(proj.at[other], raw.at[1 + half], small_s.at[2], small_r.at[2], partner),
+    ]
+    small_in = [
+        send(pot.at[:, rows_of(other)], pot_all.at[pl.ds(4 * other, 4)], small_s.at[0], small_r.at[0], partner),
+        send(info, notes.at[1 + other], small_s.at[1], small_r.at[1], partner),
+        send(proj.at[other], raw.at[1 + other], small_s.at[2], small_r.at[2], partner),
+    ]
+    cross = [
+        send(orb.at[p, rows_of(other)], e1.at[HALO + 4 * half + p, main], x_s.at[p], x_r.at[p], partner)
+        for p in range(4)
+    ]
+    cross_in = [
+        send(orb.at[p, rows_of(other)], e1.at[HALO + 4 * other + p, main], x_s.at[p], x_r.at[p], partner)
+        for p in range(4)
+    ]
+    own = [
+        send(orb.at[p, rows_of(half)], e1.at[12 * other + p, main], own_s.at[p], halo_r.at[other, p],
+             at_pair(2 * half - 1))
+        for p in range(4)
+    ]
+    forward = [
+        send(e1.at[HALO + 4 * other + p, main], e1.at[12 * half + p, main], fwd_s.at[p], halo_r.at[half, p],
+             at_pair(1 - 2 * half))
+        for p in range(4)
+    ]
+    halo_in = [
+        send(orb.at[p, rows_of(half)], e1.at[12 * side + p, main], own_s.at[p], halo_r.at[side, p], at_pair(1))
+        for side in range(2) for p in range(4)
+    ]
+    edges = [
+        send(orb.at[:, edge_rows(other, side)], e1.at[own_planes, (low, high)[side]],
+             edge_s.at[side], edge_r.at[side], partner)
+        for side in range(2)
+    ]
+    edges_in = [
+        send(orb.at[:, edge_rows(other, side)], e1.at[pl.ds(HALO + 4 * other, 4), (low, high)[side]],
+             edge_s.at[side], edge_r.at[side], partner)
+        for side in range(2)
+    ]
+    onward = [
+        send(notes.at[2], notes.at[0], next_s.at[0], next_r.at[0], at_pair(1)),
+        send(raw.at[2], raw.at[0], next_s.at[1], next_r.at[1], at_pair(1)),
+    ]
+
+    notes[1 + half] = info[...]
+    raw[1 + half] = proj[half]
+    pot_all[pl.ds(4 * half, 4)] = pot[:, rows_of(half)]
+    pl.semaphore_wait(barrier, 6)
+    for copy in small + cross + own:
+        copy.start()
+    for copy in small_in:
+        copy.wait_recv()
+    for copy in onward:
+        copy.start()
+
+    diagonal = lax.broadcasted_iota(jnp.int32, (DEPTH, DEPTH), 0) == lax.broadcasted_iota(
+        jnp.int32, (DEPTH, DEPTH), 1)
+    constant = -1.5 * center_weight - 7.0
+
+    def spread(n, carry):
+        p, r = n // ROWS, lax.rem(n, ROWS)
+        line = jnp.broadcast_to(pot_all[p, pl.ds(r, 1), :], (DEPTH, DEPTH))
+        column = jnp.sum(jnp.where(diagonal, line, 0.0), axis=1, keepdims=True)
+        shift_pot[p, r] = jnp.broadcast_to(column, (DEPTH, NORB // 4)) + constant
+        return carry
+
+    lax.fori_loop(0, PLANES * ROWS, spread, 0)
+
+    def placed(group, reach):
+        total = jnp.zeros((PROJ, CELLS), jnp.float32)
+        for k in range(SPAN):
+            flag = notes[group, :, FLAGS + reach * SPAN + k : FLAGS + reach * SPAN + k + 1]
+            total = total + flag * raw[group, :, k * CELLS : (k + 1) * CELLS]
+        return total
+
+    def store_group(group, start, slot, factor_slot):
+        for reach in range(REACH):
+            beta = placed(group, reach)
+            high_part, low_part = split(beta)
+            where = start + reach
+            left[where + 4, 2 * slot * PROJ : (2 * slot + 1) * PROJ, :] = high_part
+            left[where + 4, (2 * slot + 1) * PROJ : (2 * slot + 2) * PROJ, :] = low_part
+            if 0 <= where < PLANES:
+                wide = jnp.concatenate(
+                    [high_part.astype(jnp.float32), low_part.astype(jnp.float32), high_part.astype(jnp.float32),
+                     jnp.zeros((PROJ, CELLS), jnp.float32)], axis=0)
+                right[where, :, factor_slot * 128 : (factor_slot + 1) * 128] = wide.T.astype(jnp.bfloat16)
+
+    empty = jnp.zeros((2 * PROJ, CELLS), jnp.bfloat16)
+    for e in range(14):
+        if not 4 <= e < 10:
+            left[e, 0 : 2 * PROJ, :] = empty
+        if 6 <= e < 8:
+            left[e, 2 * PROJ :, :] = empty
+    for p in (2, 3, 6, 7):
+        right[p, :, (128 if p < 4 else 0) : (256 if p < 4 else 128)] = jnp.zeros((CELLS, 128), jnp.bfloat16)
+    store_group(1, 0, 0, 0)
+    store_group(2, 4, 1, 1)
+    for p in range(4):
+        cross_in[p].wait_recv()
+        forward[p].start()
+        if p == 2:
+            for copy in edges:
+                copy.start()
+    for copy in onward:
+        copy.wait_recv()
+    store_group(0, -4, 1, 1)
+    for copy in locals_:
+        copy.wait()
+    for copy in halo_in:
+        copy.wait_recv()
+
+    def correlate(field, phase):
+        def piece(e, total):
+            high_part, low_part = split(field[e, main].reshape(CELLS, NORB // 4))
+            both = jnp.concatenate([high_part, low_part], axis=1)
+            return total + lax.dot_general(
+                left[e], both, (((1,), (0,)), ((), ())), preferred_element_type=jnp.float32)
+
+        start = jnp.zeros((4 * PROJ, 2 * (NORB // 4)), jnp.float32)
+        first_part = lax.fori_loop(0, 8, piece, start)
+        last_part = lax.fori_loop(8, 14, piece, start)
+
+        def join(part, slot):
+            at = 2 * slot * PROJ
+            wide = part[at : at + PROJ] + part[at + PROJ : at + 2 * PROJ]
+            return wide[:, : NORB // 4] + wide[:, NORB // 4 :]
+
+        corr[phase, 0] = join(first_part, 1)
+        corr[phase, 1] = join(first_part, 0) + join(last_part, 0)
+        corr[phase, 2] = join(last_part, 1)
+        copy = send(corr.at[phase], corr_in.at[phase], corr_s.at[phase], corr_r.at[phase], partner)
+        copy.start()
+        return copy
+
+    def weigh(phase):
+        parts = []
+        for group in range(3):
+            value = corr[phase, group] + corr_in[phase, group]
+            value = dot_f32(notes[group, :, :PROJ], value, ((1,), (0,)))
+            high_part, low_part = split(value)
+            parts.append(jnp.concatenate(
+                [high_part, high_part, low_part, jnp.zeros((PROJ, NORB // 4), jnp.bfloat16)], axis=0))
+        weights[0] = jnp.concatenate([parts[1], parts[0]], axis=0)
+        weights[1] = jnp.concatenate([parts[1], parts[2]], axis=0)
+
+    def apply(field, p, scale, write):
+        product = lax.dot_general(
+            right[p], weights[p // 4], (((1,), (0,)), ((), ())), preferred_element_type=jnp.float32)
+        nonlocal_plane[...] = product.reshape(ROWS, DEPTH, NORB // 4)
+
+        def row(r, carry):
+            centre, terms = shift_terms(field, p, r)
+            total = centre * shift_pot[p, r] + nonlocal_plane[r]
+            for weight, term in zip(side_weights, terms):
+                total = total + (-0.5 * weight) * term
+            write(p, r, total * scale)
+            return carry
+
+        lax.fori_loop(0, ROWS, row, 0)
+
+    copy1 = correlate(e1, 0)
+    for copy in edges_in:
+        copy.wait_recv()
+    copy1.wait_recv()
+    weigh(0)
+
+    def write_first(p, r, value):
+        e2[p + HALO, r + HALO] = value
+
+    def halo2(p):
+        step = 2 * (p // 4) - 1
+        return send(e2.at[p + HALO, main], e2.at[lax.rem(p + 12, 16), main], y2_s.at[p], y2_r.at[p], at_pair(step))
+
+    def edge2(p, side):
+        source = pl.ds(ROWS, 4) if side == 0 else pl.ds(HALO, 4)
+        return send(e2.at[p + HALO, source], e2.at[p + HALO, (low, high)[side]],
+                    edge2_s.at[side, p], edge2_r.at[side, p], partner)
+
+    def first_plane(i, carry):
+        p = plane_order(i)
+        apply(e1, p, 1.0 / 6.0, write_first)
+        halo2(p).start()
+        edge2(p, 0).start()
+        edge2(p, 1).start()
+        return carry
+
+    lax.fori_loop(0, PLANES, first_plane, 0)
+
+    def arrive2(p, carry):
+        halo2(p).wait_recv()
+        return carry
+
+    lax.fori_loop(0, PLANES, arrive2, 0)
+    copy2 = correlate(e2, 1)
+
+    def arrive_edges(p, carry):
+        edge2(p, 0).wait_recv()
+        edge2(p, 1).wait_recv()
+        return carry
+
+    lax.fori_loop(0, PLANES, arrive_edges, 0)
+    copy2.wait_recv()
+    weigh(1)
+
+    def write_second(p, r, value):
+        second[p, r] = value - e1[p + HALO, r + HALO]
+
+    def give(p):
+        return send(second.at[p], slab.at[band, lax.rem(p, 2)], out_s.at[p], out_r.at[band, lax.rem(p, 2)],
+                    (p // 2, pair * 2 + other))
+
+    def second_plane(i, carry):
+        p = plane_order(i)
+        apply(e2, p, 1.0 / 3.0, write_second)
+        give(p).start()
+        return carry
+
+    lax.fori_loop(0, PLANES, second_plane, 0)
+
+    for b in range(4):
+        for n in range(2):
+            send(second.at[0], slab.at[b, n], out_s.at[0], out_r.at[b, n], partner).wait_recv()
+    for copy in small + cross + own + forward + edges + onward + [copy1, copy2]:
+        copy.wait_send()
+
+    def drain(p, carry):
+        halo2(p).wait_send()
+        edge2(p, 0).wait_send()
+        edge2(p, 1).wait_send()
+        give(p).wait_send()
+        return carry
+
+    lax.fori_loop(0, PLANES, drain, 0)
+
+
+def filtered_slab(orbitals, potential, projectors, info):
+    dma = pltpu.SemaphoreType.DMA
+    width = orbitals.shape[3]
+    f32, bf16 = jnp.float32, jnp.bfloat16
+    vmem = pl.BlockSpec(memory_space=pltpu.VMEM)
+    return pl.pallas_call(
+        field_kernel,
+        out_shape=jax.ShapeDtypeStruct((4, 2, ROWS, DEPTH, width), f32),
+        in_specs=[pl.BlockSpec(memory_space=pl.ANY), vmem, vmem, vmem],
+        out_specs=vmem,
+        scratch_shapes=[
+            pltpu.VMEM((PLANES + 2 * HALO, ROWS + 2 * HALO, DEPTH, width), f32),
+            pltpu.VMEM((PLANES + 2 * HALO, ROWS + 2 * HALO, DEPTH, width), f32),
+            pltpu.VMEM((PLANES, ROWS, DEPTH, width), f32),
+            pltpu.VMEM((PLANES, ROWS, DEPTH, width), f32),
+            pltpu.VMEM((ROWS, DEPTH, width), f32),
+            pltpu.VMEM((14, 4 * PROJ, CELLS), bf16),
+            pltpu.VMEM((PLANES, CELLS, 256), bf16),
+            pltpu.VMEM((3, PROJ, SPAN * CELLS), f32),
+            pltpu.VMEM((3, PROJ, 128), f32),
+            pltpu.VMEM((PLANES, ROWS, DEPTH), f32),
+            pltpu.VMEM((2, 3, PROJ, width), f32),
+            pltpu.VMEM((2, 3, PROJ, width), f32),
+            pltpu.VMEM((2, 256, width), bf16),
+            dma((3,)), dma((4,)), dma((4,)), dma((4,)), dma((4,)), dma((2, 4)), dma((2,)), dma((2,)),
+            dma((3,)), dma((3,)), dma((2,)), dma((2,)),
+            dma((2,)), dma((2,)), dma((8,)), dma((8,)), dma((2, 8)), dma((2, 8)), dma((8,)), dma((4, 2)),
+        ],
+        compiler_params=pltpu.CompilerParams(collective_id=2, has_side_effects=True, vmem_limit_bytes=58 * 2**20),
+    )(orbitals, potential, projectors, info)
+
+
+def home_kernel(result, out, local_s, send_s, recv_s):
+    band, dom = lax.axis_index("band"), lax.axis_index("dom")
+    pair, half = dom // 2, dom % 2
+    barrier = pltpu.get_barrier_semaphore()
+    for step in range(1, 8):
+        rank = lax.rem(half * 4 + band + step, 8)
+        pl.semaphore_signal(
+            barrier, inc=1, device_id=(lax.rem(rank, 4), pair * 2 + rank // 4), device_id_type=MESH)
+    pl.semaphore_wait(barrier, 7)
+    home = pair * 2 + band // 2
+    place = lax.rem(band, 2)
+    rows = 1 - half
+
+    def target(index, row_half):
+        return out.at[pl.ds(index * 2, 2), pl.ds(pl.multiple_of(row_half * ROWS, 8), ROWS)]
+
+    def move(b):
+        return pltpu.make_async_remote_copy(
+            src_ref=result.at[b], dst_ref=target(place, rows), send_sem=send_s.at[b],
+            recv_sem=recv_s.at[place, rows], device_id=(b, home), device_id_type=MESH)
+
+    local = pltpu.make_async_copy(result.at[band], target(place, rows), local_s)
+    for b in range(4):
+        mine = (b == band) & (home == dom)
+        pl.when(jnp.logical_not(mine))(lambda b=b: move(b).start())
+        pl.when(mine)(local.start)
+    for index in range(2):
+        for row_half in range(2):
+            mine = (half * 2 + index == band) & (1 - row_half == half)
+            arrival = pltpu.make_async_remote_copy(
+                src_ref=result.at[0], dst_ref=target(index, row_half), send_sem=send_s.at[0],
+                recv_sem=recv_s.at[index, row_half], device_id=(lax.rem(band + 1, 4), dom), device_id_type=MESH)
+            pl.when(jnp.logical_not(mine))(arrival.wait_recv)
+            pl.when(mine)(local.wait)
+    for b in range(4):
+        mine = (b == band) & (home == dom)
+        pl.when(jnp.logical_not(mine))(lambda b=b: move(b).wait_send())
+
+
+def send_home(result):
+    dma = pltpu.SemaphoreType.DMA
+    hbm = pl.BlockSpec(memory_space=pl.ANY)
+    return pl.pallas_call(
+        home_kernel,
+        out_shape=jax.ShapeDtypeStruct((4, 2 * ROWS, DEPTH, result.shape[-1]), jnp.float32),
+        in_specs=[hbm],
+        out_specs=hbm,
+        scratch_shapes=[dma(()), dma((4,)), dma((2, 2))],
+        compiler_params=pltpu.CompilerParams(collective_id=3, has_side_effects=True, vmem_limit_bytes=16 * 2**20),
+    )(result)
 
 
 def shards(orbitals, potential, projectors, coupling, atom_plane, projector_count):
     planes, side_y, side_z, local_orbs = orbitals.shape
-    atom_total = projectors.shape[0]
+    atoms = projectors.shape[0]
     first_plane = atom_plane - lax.axis_index("dom") * planes
-    plane_ids = jnp.arange(planes + SPAN - 1, dtype=jnp.int32)
+    reach_ids = jnp.arange(REACH, dtype=jnp.int32)
     span_ids = jnp.arange(SPAN, dtype=jnp.int32)
-    onehot = (
-        plane_ids[None, None, :] == first_plane[:, None, None] + span_ids[None, :, None]
-    ).astype(jnp.float32)
-    beta_split = projectors.reshape(atom_total, MAXPROJ, SPAN, side_y * side_z)
-    beta_full = jnp.einsum(
-        "akp,ajkc->ajpc", onehot, beta_split, precision=HIGH, preferred_element_type=jnp.float32
-    )
+    flags = (
+        reach_ids[None, :, None] == first_plane[:, None, None] + span_ids[None, None, :]
+    ).astype(jnp.float32).reshape(atoms, 1, REACH * SPAN)
+    flags = jnp.broadcast_to(flags, (atoms, MAXPROJ, REACH * SPAN)).reshape(PROJ, REACH * SPAN)
     slots = jnp.arange(MAXPROJ, dtype=jnp.int32)
     live_mask = (slots[None, :] < projector_count[:, None]).astype(jnp.float32)
     sym_coupling = 0.5 * (coupling + jnp.transpose(coupling, (0, 2, 1)))
-    layout_pieces = (beta_full, live_mask, sym_coupling)
-    first = (apply_hamiltonian(orbitals, potential, layout_pieces) - 7.0 * orbitals) / 6.0
-    second = (
-        2.0 * (apply_hamiltonian(first, potential, layout_pieces) - 7.0 * first) / 6.0 - orbitals
-    )
-    cells = planes * side_y * side_z
-    total_cells = cells * lax.axis_size("dom")
-    flat = second.reshape(cells, local_orbs)
-    panels = lax.all_gather(flat, "band", axis=1, tiled=True)
-    quarter = cells // lax.axis_size("band")
-    slab = lax.dynamic_slice_in_dim(panels, lax.axis_index("band") * quarter, quarter, 0)
-    partial_gram = jnp.dot(slab.T, slab, precision=HIGH, preferred_element_type=jnp.float32)
+    sym_coupling = sym_coupling * live_mask[:, :, None] * live_mask[:, None, :]
+    same_atom = jnp.eye(atoms, dtype=jnp.float32)
+    blocks = (sym_coupling[:, :, None, :] * same_atom[:, None, :, None]).reshape(PROJ, PROJ)
+    info = jnp.concatenate(
+        [blocks, flags, jnp.zeros((PROJ, 128 - PROJ - REACH * SPAN), jnp.float32)], axis=1)
+    halves = projectors.reshape(PROJ, SPAN, 2, CELLS).transpose(2, 0, 1, 3).reshape(2, PROJ, SPAN * CELLS)
+    slab = filtered_slab(orbitals, potential, halves, info)
+    total_cells = planes * side_y * side_z * lax.axis_size("dom")
+    flat = slab.reshape(4, 2 * CELLS, local_orbs).transpose(1, 0, 2).reshape(2 * CELLS, NORB)
+    partial_gram = jnp.dot(flat.T, flat, precision=HIGH, preferred_element_type=jnp.float32)
     gram = sum_gram(partial_gram, 1.0 / total_cells)
     inverse = inverse_factor(gram)
-    own_rows = lax.dynamic_slice_in_dim(inverse, lax.axis_index("band") * local_orbs, local_orbs, 0)
-    result = jnp.dot(panels, own_rows.T, precision=HIGH, preferred_element_type=jnp.float32)
-    return (result.reshape(planes, side_y, side_z, local_orbs), gram)
+    result = jnp.einsum(
+        "co,bpo->bcp", flat, inverse.reshape(4, local_orbs, NORB),
+        precision=HIGH, preferred_element_type=jnp.float32,
+    )
+    filtered = send_home(result.reshape(4, 2, ROWS, DEPTH, local_orbs))
+    return (filtered, gram)
 
 
 def solution(mesh):

time: 613 us -> 319 us (0.52)
  the two profiles are of different devices: /device:TPU:0 before, /device:TPU:3 now
where the time goes in v2:
time: 319 us
  Pallas kernels  276 us (87%)
  local copies, waits for them, and re-layouts  22.4 us (7%)
  matrix products  16 us (5%)
  other arithmetic  3.6 us (1%)
    pallas_call x1, Pallas kernels, filtered_slab(): pl.pallas_call(field_kernel, out_shape=jax.ShapeDtypeStruct((4, 2, ROWS,...  150 us
    pallas_call x1, Pallas kernels, send_home(): pl.pallas_call(home_kernel, out_shape=jax.ShapeDtypeStruct((4, 2 * ROWS,...  70.6 us
    pallas_call x1, Pallas kernels, sum_gram(): pl.pallas_call(functools.partial(sum_kernel, factor), out_shape=jax.Shape...  30.4 us
    pallas_call x1, Pallas kernels, inverse_factor(): pl.pallas_call(factor_kernel, out_shape=jax.ShapeDtypeStruct((size, size)...  24.8 us
    dot_general x1, matrix products, shards(): jnp.einsum('co,bpo->bcp', flat, inverse.reshape(4, local_orbs, NORB), pre...  8 us
    dot_general x1, matrix products, shards(): jnp.dot(flat.T, flat, precision=HIGH, preferred_element_type=jnp.float32)  7.97 us
    transpose x1, local copies, waits for them, and re-layouts, shards(): slab.reshape(4, 2 * CELLS, local_orbs).transpose(1, 0, 2)  7.62 us

profile of v2, /device:TPU:3, one launch (start us, length us, event | category | flops | bytes accessed | tf_op | source)
XLA Modules:
  0.0 319.1 jit_solution(1511092719070058838)
XLA Ops:
  0.6 0.7 broadcast_subtract_fusion
  1.4 0.7 fusion.6
  2.0 0.7 fusion.7
  2.7 0.8 fusion.4
  3.6 0.1 copy.15
  3.8 0.1 copy.16
  3.9 0.1 mul.51
  4.0 0.7 maximum_maximum_fusion.info
  4.7 1.6 reshape.113
  6.3 0.2 copy.26
  6.5 1.2 reshape.114.proj
  7.7 150.5 %shard_map.77 = f32[4,2,16,48,128]{4,3,2,1,0:T(8,128)} custom-call(f32[4,32,48,128]{3,2,1,0:T(8,128)} %orb.1, f32[4,32,48]{2,1,0:T(8,128)} %pot.1, f32[2,32,2304]{2,1,0:T(8,128)} %reshape.114.proj, f32[32,128]{1,0:T(8,128)} %maximum_maximum_fusion.info), custom_call_target="tpu_custom_call" | custom-call | tf_op jit(solution)/shard_map/pallas_call | solution.py:582
  158.2 8.0 %fusion.part_ref = f32[512,512]{1,0:T(8,128)S(1)} fusion(f32[4,192,8,128]{3,2,1,0:T(8,128)} %bitcast.29), kind=kOutput, calls=%fused_computation.1 | convolution fusion | flops 4831838208 | bytes 4194304 | tf_op jit(solution)/shard_map/dot_general | solution.py:683
  166.2 30.4 %shard_map.78.gram_ref = f32[512,512]{1,0:T(8,128)S(1)} custom-call(f32[512,512]{1,0:T(8,128)S(1)} %fusion.part_ref), custom_call_target="tpu_custom_call" | custom-call | tf_op jit(solution)/shard_map/pallas_call | solution.py:250
  196.7 24.8 %shard_map.79 = f32[512,512]{1,0:T(8,128)S(1)} custom-call(f32[512,512]{1,0:T(8,128)S(1)} %shard_map.78.gram_ref), custom_call_target="tpu_custom_call" | custom-call | tf_op jit(solution)/shard_map/pallas_call | solution.py:100
  221.5 1.0 copy-done
  222.5 7.6 %copy.17 = f32[1536,4,128]{2,1,0:T(4,128)} copy(f32[1536,4,128]{2,0,1:T(8,128)S(1)} %bitcast.30) | data formatting | bytes 6291456 | tf_op jit(solution)/shard_map/transpose | solution.py:682
  230.1 5.1 %reshape.120 = f32[1536,512,1]{1,0,2:T(8,128)} reshape(f32[1536,4,128]{2,1,0:T(4,128)} %copy.17) | data formatting | bytes 6291456 | tf_op jit(solution)/shard_map/reshape | solution.py:682
  235.1 8.0 %convolution_bitcast_fusion = f32[4,1536,128]{1,2,0:T(8,128)} fusion(f32[4,128,512]{2,1,0:T(8,128)S(1)} %bitcast.28, f32[1536,512,1]{1,0,2:T(8,128)} %reshape.120), kind=kOutput, calls=%fused_computation | convolution fusion | flops 4831838208 | bytes 7340032 | tf_op jit(solution)/shard_map/co,bpo->bcp/dot_general | solution.py:686
  243.1 2.4 copy.18
  245.5 70.6 %shard_map.80 = f32[4,32,48,128]{3,2,1,0:T(8,128)S(1)} custom-call(f32[4,2,16,48,128]{4,3,2,1,0:T(8,128)S(1)} %bitcast.27), custom_call_target="tpu_custom_call" | custom-call | tf_op jit(solution)/shard_map/pallas_call | solution.py:651
  316.2 1.7 copy.29
  317.8 0.3 copy-done.1
  318.1 1.0 copy.30
  (15 shorter events, 0.4 us)
Async XLA Ops:
  166.2 56.2 %copy-start.2 = (f32[4,2,16,48,128]{4,3,2,1,0:T(8,128)S(1)}, f32[4,2,16,48,128]{4,3,2,1,0:T(8,128)}, u32[]{:S(2)}) copy-start(f32[4,2,16,48,128]{4,3,2,1,0:T(8,128)} %shard_map.77) | copy-start | bytes 9437188
  221.5 1.0 copy-start
  316.2 1.9 copy-start.1

commit v3 on v1

--- a/solution.py
+++ b/solution.py
@@ -11,14 +11,13 @@
 HALO = 4
 SPAN = 3
 MAXPROJ = 4
-
+B = 128
 
 center_weight = -205.0 / 72.0
 side_weights = (8.0 / 5.0, -1.0 / 5.0, 8.0 / 315.0, -1.0 / 560.0)
 HIGH = lax.Precision.HIGHEST
 
 
-B = 128
 HIGHEST = lax.Precision.HIGHEST
 
 
@@ -109,7 +108,6 @@
 
 
 MESH = pl.DeviceIdType.MESH
-B = 128
 NEAR = 8
 FAR = 16
 SUMMERS = 10
@@ -119,11 +117,12 @@
     return [(i, j) for i in range(size // B) for j in range(i + 1)]
 
 
-def sum_kernel(factor, part_ref, gram_ref, pack, near, mine, far, total, near_s, near_r, far_s, far_r, out_s, out_r, end_s, end_r):
+def sum_kernel(factor, part_ref, gram_ref, high, low, pack, near, mine, far, total, near_s, near_r, far_s, far_r, out_s, out_r, end_s, end_r):
     band, dom = lax.axis_index("band"), lax.axis_index("dom")
     pair, half = dom // 2, dom % 2
     rank = half * 4 + band
-    blocks = tri_blocks(part_ref.shape[0])
+    size = part_ref.shape[1]
+    blocks = tri_blocks(size)
     share = len(blocks) * B // NEAR
     piece = share // SUMMERS
 
@@ -140,8 +139,22 @@
         pl.semaphore_signal(barrier, inc=1, device_id=near_peer(step)[1], device_id_type=MESH)
     for step in range(1, FAR):
         pl.semaphore_signal(barrier, inc=1, device_id=far_peer(step)[1], device_id_type=MESH)
-    for n, (i, j) in enumerate(blocks):
-        pack[n * B : (n + 1) * B, :] = part_ref[i * B : (i + 1) * B, j * B : (j + 1) * B]
+    contract = (((0,), (0,)), ((), ()))
+
+    def split_rows(n, carry):
+        at = pl.ds(pl.multiple_of(n * 128, 128), 128)
+        high[at, :], low[at, :] = split(part_ref[at, :])
+        return carry
+
+    lax.fori_loop(0, part_ref.shape[0] // 128, split_rows, 0)
+    for i in range(size // B):
+        own, wide = slice(i * B, (i + 1) * B), slice(0, (i + 1) * B)
+        block_row = lax.dot_general(high[:, own], high[:, wide], contract, preferred_element_type=jnp.float32)
+        block_row += lax.dot_general(high[:, own], low[:, wide], contract, preferred_element_type=jnp.float32)
+        block_row += lax.dot_general(low[:, own], high[:, wide], contract, preferred_element_type=jnp.float32)
+        for j in range(i + 1):
+            n = blocks.index((i, j))
+            pack[n * B : (n + 1) * B, :] = block_row[:, j * B : (j + 1) * B]
     pl.semaphore_wait(barrier, NEAR + FAR - 2)
 
     def rows(index, count):
@@ -245,7 +258,7 @@
 
 
 def sum_gram(part, factor):
-    size = part.shape[0]
+    cells, size = part.shape
     packed = len(tri_blocks(size)) * B
     share = packed // NEAR
     dma = pltpu.SemaphoreType.DMA
@@ -255,6 +268,8 @@
         in_specs=[pl.BlockSpec(memory_space=pltpu.VMEM)],
         out_specs=pl.BlockSpec(memory_space=pltpu.VMEM),
         scratch_shapes=[
+            pltpu.VMEM((cells, size), jnp.bfloat16),
+            pltpu.VMEM((cells, size), jnp.bfloat16),
             pltpu.VMEM((packed, B), jnp.float32),
             pltpu.VMEM((NEAR, share, B), jnp.float32),
             pltpu.VMEM((share, B), jnp.float32),
@@ -267,109 +282,535 @@
     )(part)
 
 
-def with_halo(value, sides, width):
-    for axis, dim in sides:
-        peers, length = (lax.axis_size(axis), value.shape[dim])
-        up = [(i, (i + 1) % peers) for i in range(peers)]
-        down = [(j, i) for i, j in up]
-        last = lax.slice_in_dim(value, length - width, length, axis=dim)
-        first = lax.slice_in_dim(value, 0, width, axis=dim)
-        before = lax.ppermute(last, axis, up)
-        after = lax.ppermute(first, axis, down)
-        value = jnp.concatenate([before, value, after], axis=dim)
-    return value
-
-
-def passed_along(value, axis, steps):
-    count = lax.axis_size(axis)
-    pairs = [(source, (source + steps) % count) for source in range(count)]
-    return lax.ppermute(value, axis, pairs)
-
-
-def laplacian(orbital_field, padded, planes):
-    total = 3.0 * center_weight * orbital_field
-    for offset in range(1, 5):
-        weight = side_weights[offset - 1]
-        total = total + weight * (
-            padded[HALO + offset : HALO + offset + planes]
-            + padded[HALO - offset : HALO - offset + planes]
+ROWS = 32
+DEPTH = 48
+WIDE = 128
+CELLS = ROWS * DEPTH
+PROJ = 32
+REACH = 6
+FLAGS = PROJ
+GROUP = 8
+STRIP = 8
+STRIPS = ROWS // STRIP
+PIECE = 4
+PIECES = ROWS // PIECE
+AREA = STRIP * DEPTH
+
+
+def split(value):
+    high = value.astype(jnp.bfloat16)
+    return high, (value - high.astype(jnp.float32)).astype(jnp.bfloat16)
+
+
+def swap(value):
+    return pltpu.roll(value, WIDE // 2, value.ndim - 1)
+
+
+def field_kernel(
+    orb, pot, proj, info, out,
+    e1, e2, second, shift_pot, nonlocal_plane, left, right, raw, notes, pot_all, corr, corr_in, weights,
+    give_cross, give_keep, got_cross, got1, got2, slab,
+    local_s, x_s, x_r, own_s, fwd_s, halo_r, small_s, small_r, core_s, core_r, next_s, next_r, last_s, last_r,
+    corr_s, corr_r, y2_s, y2_r, out_s, out_r, self_s,
+):
+    band, dom = lax.axis_index("band"), lax.axis_index("dom")
+    pair, half = dom // 2, dom % 2
+    other = 1 - half
+    core = lax.rem(band, 2)
+    rank = half * 4 + band
+    pairs = lax.axis_size("dom") // 2
+    partner = (band, pair * 2 + other)
+    sibling = (band + 1 - 2 * core, dom)
+
+    def at_pair(step):
+        return (band, lax.rem(pair + step + pairs, pairs) * 2 + half)
+
+    def send(src, dst, ssem, rsem, device):
+        return pltpu.make_async_remote_copy(
+            src_ref=src, dst_ref=dst, send_sem=ssem, recv_sem=rsem, device_id=device, device_id_type=MESH)
+
+    def member(index):
+        return (lax.rem(index, 4), pair * 2 + index // 4)
+
+    barrier = pltpu.get_barrier_semaphore()
+    for peer in [at_pair(1), at_pair(-1)] + [member(lax.rem(rank + n, GROUP)) for n in range(1, GROUP)]:
+        pl.semaphore_signal(barrier, inc=1, device_id=peer, device_id_type=MESH)
+
+    loads = [pltpu.make_async_copy(orb.at[p], second.at[p], local_s.at[p]) for p in range(4)]
+    for copy in loads:
+        copy.start()
+    lane = lax.broadcasted_iota(jnp.int32, (DEPTH, WIDE), 1)
+    lower = lane < WIDE // 2
+    kept = (lane // (WIDE // 2)) == half
+
+    share = pl.ds(pl.multiple_of(core * (PROJ // 2), 16), PROJ // 2)
+    twin = pl.ds(pl.multiple_of((1 - core) * (PROJ // 2), 16), PROJ // 2)
+    small = [
+        send(pot, pot_all.at[pl.ds(4 * half, 4)], small_s.at[0], small_r.at[0], partner),
+        send(info, notes.at[1 + half], small_s.at[1], small_r.at[1], partner),
+        send(proj.at[share], raw.at[1 + half, share], small_s.at[2], small_r.at[2], partner),
+    ]
+    small_in = [
+        send(pot, pot_all.at[pl.ds(4 * other, 4)], small_s.at[0], small_r.at[0], partner),
+        send(info, notes.at[1 + other], small_s.at[1], small_r.at[1], partner),
+        send(proj.at[share], raw.at[1 + other, share], small_s.at[2], small_r.at[2], partner),
+    ]
+    across = send(raw.at[1 + other, share], raw.at[1 + other, share], core_s, core_r, sibling)
+    across_in = send(raw.at[1 + other, twin], raw.at[1 + other, twin], core_s, core_r, sibling)
+    onward = [
+        send(notes.at[2], notes.at[0], next_s.at[0], next_r.at[0], at_pair(1)),
+        send(raw.at[2, share], raw.at[0, share], next_s.at[1], next_r.at[1], at_pair(1)),
+    ]
+    last = send(raw.at[0, share], raw.at[0, share], last_s, last_r, sibling)
+    last_in = send(raw.at[0, twin], raw.at[0, twin], last_s, last_r, sibling)
+
+    def piece_rows(c):
+        return pl.ds(c * PIECE, PIECE)
+
+    def cross(c):
+        at = (slice(None), piece_rows(c))
+        return send(give_cross.at[at], got_cross.at[at], x_s.at[c], x_r.at[c], partner)
+
+    def keep(c):
+        at = piece_rows(c)
+        return send(give_keep.at[:, at], got1.at[other, :, at], own_s.at[c], halo_r.at[other, c],
+                    at_pair(2 * half - 1))
+
+    def forward(c):
+        at = piece_rows(c)
+        return send(got_cross.at[:, at], got1.at[half, :, at], fwd_s.at[c], halo_r.at[half, c],
+                    at_pair(1 - 2 * half))
+
+    def halo_in(side, c):
+        at = piece_rows(c)
+        return send(give_keep.at[:, at], got1.at[side, :, at], own_s.at[c], halo_r.at[side, c], at_pair(1))
+
+    notes[1 + half] = info[...]
+    raw[1 + half] = proj[...]
+    pot_all[pl.ds(4 * half, 4)] = pot[...]
+    for copy in loads:
+        copy.wait()
+    pl.semaphore_wait(barrier, GROUP + 1)
+    for copy in small:
+        copy.start()
+
+    def pack_piece(c, carry):
+        for n in range(PIECE):
+            r = c * PIECE + n
+            for j in range(2):
+                near, far = second[j, r], second[j + 2, r]
+                give_cross[j, r] = jnp.where(kept, swap(near), far)
+                give_keep[j, r] = jnp.where(kept, near, swap(far))
+        cross(c).start()
+        keep(c).start()
+        return carry
+
+    lax.fori_loop(0, PIECES, pack_piece, 0)
+
+    for copy in small_in:
+        copy.wait_recv()
+    across.start()
+    for copy in onward[:1]:
+        copy.start()
+
+    def placed(group, reach):
+        total = jnp.zeros((PROJ, CELLS), jnp.float32)
+        for k in range(SPAN):
+            flag = notes[group, :, FLAGS + reach * SPAN + k : FLAGS + reach * SPAN + k + 1]
+            total = total + flag * raw[group, :, k * CELLS : (k + 1) * CELLS]
+        return total
+
+    def store_pair(p, groups, reach, slot):
+        beta = jnp.concatenate([placed(group, reach) for group in groups], axis=0)
+        high_part, low_part = split(beta)
+        both = jnp.concatenate([high_part, low_part], axis=0)
+        for n in range(STRIPS):
+            left[p, n, slot * 128 : (slot + 1) * 128, :] = both[:, n * AREA : (n + 1) * AREA]
+        high32 = high_part.astype(jnp.float32)
+        wide = jnp.concatenate([high32, low_part.astype(jnp.float32)], axis=0)
+        turned = wide.T.astype(jnp.bfloat16)
+        right[p, :, slot * 256 : slot * 256 + 128] = turned
+        right[p, :, slot * 256 + 128 : slot * 256 + 192] = turned[:, :64]
+        right[p, :, slot * 256 + 192 : slot * 256 + 256] = jnp.zeros((CELLS, 64), jnp.bfloat16)
+
+    diagonal = lax.broadcasted_iota(jnp.int32, (DEPTH, DEPTH), 0) == lax.broadcasted_iota(
+        jnp.int32, (DEPTH, DEPTH), 1)
+    constant = -1.5 * center_weight - 7.0
+
+    def spread(n, carry):
+        p, r = n // ROWS, lax.rem(n, ROWS)
+        columns = []
+        for extra in (0, 4):
+            line = jnp.broadcast_to(pot_all[p + extra, pl.ds(r, 1), :], (DEPTH, DEPTH))
+            columns.append(jnp.sum(jnp.where(diagonal, line, 0.0), axis=1, keepdims=True))
+        shift_pot[p, r] = jnp.where(lower, columns[0], columns[1]) + constant
+        return carry
+
+    def receive_piece(c):
+        cross(c).wait_recv()
+        forward(c).start()
+
+        def one(n, carry):
+            r = c * PIECE + n
+            for j in range(2):
+                arrived = got_cross[j, r]
+                e1[4 + j, r] = jnp.where(kept, second[j, r], arrived)
+                e1[6 + j, r] = jnp.where(kept, second[j + 2, r], swap(arrived))
+            return carry
+
+        lax.fori_loop(0, PIECE, one, 0)
+
+    for p in (2, 3):
+        left[p, :, 128:256, :] = jnp.zeros((STRIPS, 128, AREA), jnp.bfloat16)
+        right[p, :, 256:512] = jnp.zeros((CELLS, 256), jnp.bfloat16)
+    lax.fori_loop(0, 64, spread, 0)
+    across_in.wait_recv()
+    onward[1].start()
+    receive_piece(0)
+    store_pair(0, (1, 2), 0, 0)
+    store_pair(1, (1, 2), 1, 0)
+    receive_piece(1)
+    store_pair(2, (1, 2), 2, 0)
+    store_pair(3, (1, 2), 3, 0)
+    receive_piece(2)
+    for copy in onward:
+        copy.wait_recv()
+    last.start()
+    lax.fori_loop(64, 4 * ROWS, spread, 0)
+    receive_piece(3)
+    last_in.wait_recv()
+    store_pair(0, (0, 1), 4, 1)
+    store_pair(1, (0, 1), 5, 1)
+    for c in range(4, PIECES):
+        receive_piece(c)
+
+    def correlate(field, phase):
+        def part(n, total):
+            p, strip = n // STRIPS, lax.rem(n, STRIPS)
+            cells = field[4 + p, pl.ds(strip * STRIP, STRIP)].reshape(AREA, WIDE)
+            both = jnp.concatenate(split(cells), axis=1)
+            return total + lax.dot_general(
+                left[p, strip], both, (((1,), (0,)), ((), ())), preferred_element_type=jnp.float32)
+
+        total = lax.fori_loop(0, 4 * STRIPS, part, jnp.zeros((256, 2 * WIDE), jnp.float32))
+        total = total[:, :WIDE] + total[:, WIDE:]
+        near, tail = total[0:64] + total[64:128], total[128:192] + total[192:256]
+        corr[phase, 0] = tail[:PROJ]
+        corr[phase, 1] = near[PROJ:]
+        corr[phase, 2] = near[:PROJ] + swap(tail[PROJ:])
+        down = send(corr.at[phase, 0], corr_in.at[phase, 1], corr_s.at[phase, 0], corr_r.at[phase, 1], at_pair(-1))
+        up = send(corr.at[phase, 1], corr_in.at[phase, 0], corr_s.at[phase, 1], corr_r.at[phase, 0], at_pair(1))
+        down.start()
+        up.start()
+        return [down, up]
+
+    def weigh(phase, copies):
+        for copy in copies:
+            copy.wait_recv()
+        before = corr[phase, 0] + swap(corr_in[phase, 0])
+        after = corr[phase, 1] + swap(corr_in[phase, 1])
+        before, own, after = (
+            dot_f32(notes[group, :, :PROJ], value, ((1,), (0,)))
+            for group, value in ((0, before), (1, corr[phase, 2]), (2, after))
         )
-        total = total + weight * (
-            jnp.roll(orbital_field, offset, 1) + jnp.roll(orbital_field, -offset, 1)
-        )
-        total = total + weight * (
-            jnp.roll(orbital_field, offset, 2) + jnp.roll(orbital_field, -offset, 2)
-        )
-    return total
-
-
-def apply_hamiltonian(orbital_field, potential, layout_pieces):
-    planes, side_y, side_z, local_orbs = orbital_field.shape
-    beta_full, live_mask, sym_coupling = layout_pieces
-    padded = with_halo(orbital_field, (("dom", 0),), HALO)
-    extended = padded[HALO : HALO + planes + SPAN - 1].reshape(
-        planes + SPAN - 1, side_y * side_z, local_orbs
-    )
-    correlations = (
-        jnp.einsum(
-            "ajpc,pco->ajo", beta_full, extended, precision=HIGH, preferred_element_type=jnp.float32
-        )
-        * live_mask[:, :, None]
-    )
-    weighted = (
-        jnp.einsum(
-            "aij,ajo->aio",
-            sym_coupling,
-            correlations,
-            precision=HIGH,
-            preferred_element_type=jnp.float32,
-        )
-        * live_mask[:, :, None]
-    )
-    contrib = jnp.einsum(
-        "ajpc,ajo->pco", beta_full, weighted, precision=HIGH, preferred_element_type=jnp.float32
-    )
-    contrib = contrib.reshape(planes + SPAN - 1, side_y, side_z, local_orbs)
-    arrived = passed_along(contrib[planes:], "dom", 1)
-    own_planes = contrib[:planes]
-    own_planes = jnp.concatenate([own_planes[: SPAN - 1] + arrived, own_planes[SPAN - 1 :]], axis=0)
-    kinetic = -0.5 * laplacian(orbital_field, padded, planes)
-    return kinetic + potential[:, :, :, None] * orbital_field + own_planes
+        in_low = lax.broadcasted_iota(jnp.int32, (PROJ, WIDE), 1) < WIDE // 2
+        zero = jnp.zeros((64, WIDE), jnp.bfloat16)
+        parts = []
+        for low_value, high_value in ((own, after), (before, swap(own))):
+            value = jnp.concatenate(
+                [jnp.where(in_low, low_value, 0.0), jnp.where(in_low, 0.0, high_value)], axis=0)
+            high_part, low_part = split(value)
+            parts += [high_part, high_part, low_part, zero]
+        weights[...] = jnp.concatenate(parts, axis=0)
+
+    def open_strip(field, got, strip):
+        def one(n, carry):
+            r = strip * STRIP + n
+            for j in range(2):
+                near, far = field[4 + j, r], field[6 + j, r]
+                up, down = got[0, j, r], got[1, j, r]
+                field[j, r] = swap(jnp.where(lower, near, up))
+                field[2 + j, r] = jnp.where(lower, up, swap(far))
+                field[8 + j, r] = swap(jnp.where(lower, down, near))
+                field[10 + j, r] = jnp.where(lower, swap(far), down)
+            return carry
+
+        lax.fori_loop(0, STRIP, one, 0)
+
+    def apply(field, strip, scale, write):
+        def plane(p, carry):
+            product = lax.dot_general(
+                right[p, pl.ds(pl.multiple_of(strip * AREA, AREA), AREA), :], weights[...],
+                (((1,), (0,)), ((), ())), preferred_element_type=jnp.float32)
+            nonlocal_plane[...] = product.reshape(STRIP, DEPTH, WIDE)
+
+            def row(n, inner):
+                r = strip * STRIP + n
+                centre = field[p + 4, r]
+                total = centre * shift_pot[p, r] + nonlocal_plane[n]
+                for k in range(1, 5):
+                    pair_x = field[p + 4 + k, r] + field[p + 4 - k, r]
+                    pair_y = field[p + 4, lax.rem(r + k, ROWS)] + field[p + 4, lax.rem(r + ROWS - k, ROWS)]
+                    pair_z = pltpu.roll(centre, k, 0) + pltpu.roll(centre, DEPTH - k, 0)
+                    total = total + (-0.5 * side_weights[k - 1]) * ((pair_x + pair_y) + pair_z)
+                write(p, r, total * scale)
+                return inner
+
+            lax.fori_loop(0, STRIP, row, 0)
+            return carry
+
+        lax.fori_loop(0, 4, plane, 0)
+
+    copies1 = correlate(e1, 0)
+
+    def halo_strip(strip, carry):
+        for side in range(2):
+            for n in range(STRIP // PIECE):
+                halo_in(side, strip * (STRIP // PIECE) + n).wait_recv()
+        open_strip(e1, got1, strip)
+        return carry
+
+    lax.fori_loop(0, STRIPS, halo_strip, 0)
+
+    def sent_piece(c, carry):
+        cross(c).wait_send()
+        keep(c).wait_send()
+        forward(c).wait_send()
+        return carry
+
+    lax.fori_loop(0, PIECES, sent_piece, 0)
+    weigh(0, copies1)
+
+    def write_first(p, r, value):
+        e2[p + 4, r] = value
+
+    def strip_rows(strip):
+        return pl.ds(strip * STRIP, STRIP)
+
+    def up2(strip):
+        at = strip_rows(strip)
+        return send(give_cross.at[:, at], got2.at[0, :, at], y2_s.at[0, strip], y2_r.at[0, strip], at_pair(1))
+
+    def down2(strip):
+        at = strip_rows(strip)
+        return send(give_keep.at[:, at], got2.at[1, :, at], y2_s.at[1, strip], y2_r.at[1, strip], at_pair(-1))
+
+    def first_strip(strip, carry):
+        apply(e1, strip, 1.0 / 6.0, write_first)
+
+        def pack(n, inner):
+            r = strip * STRIP + n
+            for j in range(2):
+                near, turned = e2[4 + j, r], swap(e2[6 + j, r])
+                give_cross[j, r] = jnp.where(lower, turned, near)
+                give_keep[j, r] = jnp.where(lower, near, turned)
+            return inner
+
+        lax.fori_loop(0, STRIP, pack, 0)
+        up2(strip).start()
+        down2(strip).start()
+        return carry
+
+    lax.fori_loop(0, STRIPS, first_strip, 0)
+    copies2 = correlate(e2, 1)
+    weigh(1, copies2)
+
+    def write_second(p, r, value):
+        second[p, r] = value - e1[p + 4, r]
+
+    def give(index, part):
+        src = second.at[index // 2, pl.ds(lax.rem(index, 2) * 16 + part * STRIP, STRIP)]
+        return send(src, slab.at[rank, pl.ds(part * STRIP, STRIP)], out_s.at[index, part], out_r.at[rank, part],
+                    member(index))
+
+    def own_part(part):
+        src = second.at[rank // 2, pl.ds(lax.rem(rank, 2) * 16 + part * STRIP, STRIP)]
+        return pltpu.make_async_copy(src, slab.at[rank, pl.ds(part * STRIP, STRIP)], self_s.at[part])
+
+    def second_strip(strip, carry):
+        up2(strip).wait_recv()
+        down2(strip).wait_recv()
+        open_strip(e2, got2, strip)
+        apply(e2, strip, 1.0 / 3.0, write_second)
+        part = lax.rem(strip, 2)
+        for n in range(4):
+            index = 2 * lax.rem(n + rank // 2 + 2, 4) + strip // 2
+            pl.when(index != rank)(lambda index=index: give(index, part).start())
+        pl.when(lax.rem(rank, 2) == strip // 2)(own_part(part).start)
+        return carry
+
+    lax.fori_loop(0, STRIPS, second_strip, 0)
+
+    for n in range(1, GROUP):
+        index = lax.rem(rank + n, GROUP)
+        for part in range(2):
+            send(second.at[0, pl.ds(0, STRIP)], slab.at[index, pl.ds(part * STRIP, STRIP)], out_s.at[index, part],
+                 out_r.at[index, part], member(index)).wait_recv()
+    own_part(0).wait()
+    own_part(1).wait()
+
+    def repack(n, carry):
+        cells = pl.ds(pl.multiple_of(n * DEPTH, 8), DEPTH)
+        more = pl.ds(pl.multiple_of(CELLS // 2 + n * DEPTH, 8), DEPTH)
+        for b in range(4):
+            at = slice(b * WIDE, (b + 1) * WIDE)
+            here, there = slab[b, n], slab[4 + b, n]
+            out[cells, at] = jnp.where(lower, here, swap(there))
+            out[more, at] = jnp.where(lower, swap(here), there)
+        return carry
+
+    lax.fori_loop(0, ROWS // 2, repack, 0)
+
+    for copy in small + [across, last] + onward + copies1 + copies2:
+        copy.wait_send()
+    for strip in range(STRIPS):
+        up2(strip).wait_send()
+        down2(strip).wait_send()
+    for n in range(1, GROUP):
+        for part in range(2):
+            give(lax.rem(rank + n, GROUP), part).wait_send()
+
+
+def filtered_slab(orbitals, potential, projectors, info):
+    dma = pltpu.SemaphoreType.DMA
+    f32, bf16 = jnp.float32, jnp.bfloat16
+    vmem = pl.BlockSpec(memory_space=pltpu.VMEM)
+    block = (ROWS, DEPTH, WIDE)
+    return pl.pallas_call(
+        field_kernel,
+        out_shape=jax.ShapeDtypeStruct((CELLS, NORB), f32),
+        in_specs=[pl.BlockSpec(memory_space=pl.ANY), vmem, vmem, vmem],
+        out_specs=vmem,
+        scratch_shapes=[
+            pltpu.VMEM((12,) + block, f32),
+            pltpu.VMEM((12,) + block, f32),
+            pltpu.VMEM((4,) + block, f32),
+            pltpu.VMEM((4,) + block, f32),
+            pltpu.VMEM((STRIP, DEPTH, WIDE), f32),
+            pltpu.VMEM((4, STRIPS, 256, AREA), bf16),
+            pltpu.VMEM((4, CELLS, 512), bf16),
+            pltpu.VMEM((3, PROJ, SPAN * CELLS), f32),
+            pltpu.VMEM((3, PROJ, 128), f32),
+            pltpu.VMEM((8, ROWS, DEPTH), f32),
+            pltpu.VMEM((2, 3, PROJ, WIDE), f32),
+            pltpu.VMEM((2, 2, PROJ, WIDE), f32),
+            pltpu.VMEM((512, WIDE), bf16),
+            pltpu.VMEM((2,) + block, f32),
+            pltpu.VMEM((2,) + block, f32),
+            pltpu.VMEM((2,) + block, f32),
+            pltpu.VMEM((2, 2) + block, f32),
+            pltpu.VMEM((2, 2) + block, f32),
+            pltpu.VMEM((GROUP, ROWS // 2, DEPTH, WIDE), f32),
+            dma((4,)), dma((PIECES,)), dma((PIECES,)), dma((PIECES,)), dma((PIECES,)), dma((2, PIECES)),
+            dma((3,)), dma((3,)), dma(()), dma(()), dma((2,)), dma((2,)), dma(()), dma(()),
+            dma((2, 2)), dma((2, 2)), dma((2, STRIPS)), dma((2, STRIPS)),
+            dma((GROUP, 2)), dma((GROUP, 2)), dma((2,)),
+        ],
+        compiler_params=pltpu.CompilerParams(collective_id=2, has_side_effects=True, vmem_limit_bytes=62 * 2**20),
+    )(orbitals, potential, projectors, info)
+
+
+def home_kernel(flat, inverse, out, parts, turned, local_s, send_s, recv_s):
+    band, dom = lax.axis_index("band"), lax.axis_index("dom")
+    pair, half = dom // 2, dom % 2
+    rank = half * 4 + band
+    place, core = (band // 2) * 2 + half, lax.rem(band, 2)
+    barrier = pltpu.get_barrier_semaphore()
+    for step in range(1, GROUP):
+        index = lax.rem(rank + step, GROUP)
+        pl.semaphore_signal(
+            barrier, inc=1, device_id=(lax.rem(index, 4), pair * 2 + index // 4), device_id_type=MESH)
+    high_part, low_part = split(inverse[...])
+    turned[0], turned[1] = high_part, low_part
+
+    def target(index):
+        return out.at[index // 2, pl.ds(pl.multiple_of(lax.rem(index, 2) * 16, 8), ROWS // 2)]
+
+    def choice(n):
+        chip = lax.rem(place + (2, 1, 3, 0)[n // 2], 4)
+        return lax.rem(chip, 2), (chip // 2) * 2 + lax.rem(core + 1 + n, 2)
+
+    def move(n):
+        to_half, to_band = choice(n)
+        return pltpu.make_async_remote_copy(
+            src_ref=parts.at[n], dst_ref=target(rank), send_sem=send_s.at[n], recv_sem=recv_s.at[rank],
+            device_id=(to_band, pair * 2 + to_half), device_id_type=MESH)
+
+    local = pltpu.make_async_copy(parts.at[GROUP - 1], target(rank), local_s)
+    contract = (((1,), (1,)), ((), ()))
+    for n in range(GROUP):
+        to_half, to_band = choice(n)
+        rows = pl.ds(pl.multiple_of(to_band * B, B), B)
+
+        def tile(m, carry, n=n, to_half=to_half, rows=rows):
+            size = CELLS // 8
+            cells = flat[pl.ds(pl.multiple_of(to_half * (CELLS // 2) + m * size, 8), size), :]
+            high_cells, low_cells = split(cells)
+            high_rot, low_rot = turned[0, rows, :], turned[1, rows, :]
+            both = jnp.concatenate([high_rot, low_rot], axis=0)
+            wide = lax.dot_general(high_cells, both, contract, preferred_element_type=jnp.float32)
+            more = lax.dot_general(low_cells, high_rot, contract, preferred_element_type=jnp.float32)
+            value = wide[:, :B] + (wide[:, B:] + more)
+            parts[n, pl.ds(m * (size // DEPTH), size // DEPTH)] = value.reshape(size // DEPTH, DEPTH, WIDE)
+            return carry
+
+        lax.fori_loop(0, 4, tile, 0)
+        if n == 0:
+            pl.semaphore_wait(barrier, GROUP - 1)
+        if n < GROUP - 1:
+            move(n).start()
+        else:
+            local.start()
+    for step in range(1, GROUP):
+        index = lax.rem(rank + step, GROUP)
+        pltpu.make_async_remote_copy(
+            src_ref=parts.at[0], dst_ref=target(index), send_sem=send_s.at[0], recv_sem=recv_s.at[index],
+            device_id=(lax.rem(index, 4), pair * 2 + index // 4), device_id_type=MESH).wait_recv()
+    local.wait()
+    for n in range(GROUP - 1):
+        move(n).wait_send()
+
+
+def rotate_home(flat, inverse):
+    dma = pltpu.SemaphoreType.DMA
+    vmem = pl.BlockSpec(memory_space=pltpu.VMEM)
+    return pl.pallas_call(
+        home_kernel,
+        out_shape=jax.ShapeDtypeStruct((4, ROWS, DEPTH, WIDE), jnp.float32),
+        in_specs=[vmem, vmem],
+        out_specs=pl.BlockSpec(memory_space=pl.ANY),
+        scratch_shapes=[
+            pltpu.VMEM((GROUP, ROWS // 2, DEPTH, WIDE), jnp.float32),
+            pltpu.VMEM((2, NORB, NORB), jnp.bfloat16),
+            dma(()), dma((GROUP,)), dma((GROUP,)),
+        ],
+        compiler_params=pltpu.CompilerParams(collective_id=3, has_side_effects=True, vmem_limit_bytes=40 * 2**20),
+    )(flat, inverse)
 
 
 def shards(orbitals, potential, projectors, coupling, atom_plane, projector_count):
     planes, side_y, side_z, local_orbs = orbitals.shape
-    atom_total = projectors.shape[0]
+    atoms = projectors.shape[0]
     first_plane = atom_plane - lax.axis_index("dom") * planes
-    plane_ids = jnp.arange(planes + SPAN - 1, dtype=jnp.int32)
+    reach_ids = jnp.arange(REACH, dtype=jnp.int32)
     span_ids = jnp.arange(SPAN, dtype=jnp.int32)
-    onehot = (
-        plane_ids[None, None, :] == first_plane[:, None, None] + span_ids[None, :, None]
-    ).astype(jnp.float32)
-    beta_split = projectors.reshape(atom_total, MAXPROJ, SPAN, side_y * side_z)
-    beta_full = jnp.einsum(
-        "akp,ajkc->ajpc", onehot, beta_split, precision=HIGH, preferred_element_type=jnp.float32
-    )
+    flags = (
+        reach_ids[None, :, None] == first_plane[:, None, None] + span_ids[None, None, :]
+    ).astype(jnp.float32).reshape(atoms, 1, REACH * SPAN)
+    flags = jnp.broadcast_to(flags, (atoms, MAXPROJ, REACH * SPAN)).reshape(PROJ, REACH * SPAN)
     slots = jnp.arange(MAXPROJ, dtype=jnp.int32)
     live_mask = (slots[None, :] < projector_count[:, None]).astype(jnp.float32)
     sym_coupling = 0.5 * (coupling + jnp.transpose(coupling, (0, 2, 1)))
-    layout_pieces = (beta_full, live_mask, sym_coupling)
-    first = (apply_hamiltonian(orbitals, potential, layout_pieces) - 7.0 * orbitals) / 6.0
-    second = (
-        2.0 * (apply_hamiltonian(first, potential, layout_pieces) - 7.0 * first) / 6.0 - orbitals
-    )
-    cells = planes * side_y * side_z
-    total_cells = cells * lax.axis_size("dom")
-    flat = second.reshape(cells, local_orbs)
-    panels = lax.all_gather(flat, "band", axis=1, tiled=True)
-    quarter = cells // lax.axis_size("band")
-    slab = lax.dynamic_slice_in_dim(panels, lax.axis_index("band") * quarter, quarter, 0)
-    partial_gram = jnp.dot(slab.T, slab, precision=HIGH, preferred_element_type=jnp.float32)
-    gram = sum_gram(partial_gram, 1.0 / total_cells)
-    inverse = inverse_factor(gram)
-    own_rows = lax.dynamic_slice_in_dim(inverse, lax.axis_index("band") * local_orbs, local_orbs, 0)
-    result = jnp.dot(panels, own_rows.T, precision=HIGH, preferred_element_type=jnp.float32)
-    return (result.reshape(planes, side_y, side_z, local_orbs), gram)
+    sym_coupling = sym_coupling * live_mask[:, :, None] * live_mask[:, None, :]
+    same_atom = jnp.eye(atoms, dtype=jnp.float32)
+    blocks = (sym_coupling[:, :, None, :] * same_atom[:, None, :, None]).reshape(PROJ, PROJ)
+    info = jnp.concatenate(
+        [blocks, flags, jnp.zeros((PROJ, 128 - PROJ - REACH * SPAN), jnp.float32)], axis=1)
+    flat = filtered_slab(orbitals, potential, projectors.reshape(PROJ, SPAN * CELLS), info)
+    total_cells = planes * side_y * side_z * lax.axis_size("dom")
+    gram = sum_gram(flat, 1.0 / total_cells)
+    filtered = rotate_home(flat, inverse_factor(gram))
+    return (filtered, gram)
 
 
 def solution(mesh):

time: 613 us -> 270 us (0.44); the launches traced: 601 us -> 269 us
  waiting for transfers between devices: 340 us -> 0 us
  Pallas kernels: 56.6 us -> 257 us
  local copies, waits for them, and re-layouts: 75.3 us -> 7.06 us
  other arithmetic: 57.4 us -> 3.6 us
  matrix products: 46.1 us -> 0 us
  between operations: 14.4 us -> 0.71 us
  starting transfers between devices: 11.5 us -> 0 us
    ppermute x6 -> x0, waiting for transfers between devices: 255 us -> none  [the longest x2 108 us: with_halo(): after = lax.ppermute(first, axis, down)]
    pallas_call x0 -> x2, Pallas kernels: none -> 188 us  [the longest x1 149 us: filtered_slab(): pl.pallas_call(field_kernel, out_shape=jax.ShapeDtypeStruct((CELLS, NORB)...]
    all_gather x1 -> x0, waiting for transfers between devices: 85.4 us -> none  [shards(): panels = lax.all_gather(flat, 'band', axis=1, tiled=True)]
    slice x35 -> x0, local copies, waits for them, and re-layouts: 65.2 us -> none  [the longest x16 31.1 us: laplacian(): jnp.roll(orbital_field, offset, 1) + jnp.roll(orbital_field, -offset, 1)]
    dot_general x9 -> x0, matrix products: 46.1 us -> none  [the longest x2 15.6 us: apply_hamiltonian(): jnp.einsum('ajpc,ajo->pco', beta_full, weighted, precision=HIGH, preferre...]
    div x1 -> x0, other arithmetic: 28.9 us -> none  [shards(): (apply_hamiltonian(orbitals, potential, layout_pieces) - 7.0 * orbitals)...]
    sub x1 -> x0, other arithmetic: 24.7 us -> none  [shards(): 2.0 * (apply_hamiltonian(first, potential, layout_pieces) - 7.0 * first)]
    pallas_call x1, Pallas kernels: 31.9 us -> 45.1 us  [sum_gram(): pl.pallas_call(functools.partial(sum_kernel, factor), out_shape=jax.Shape...]
  transfers between devices with their start and end apart: 7 -> 0, of which waited for: 6 -> 0; matrix products, arithmetic and copies ran while one was open for 14% -> 0% of each run, Pallas kernels for 0% -> 0%
where the time goes in v3:
time: 270 us; the launch traced here: 269 us
  Pallas kernels  257 us (95%)
  local copies, waits for them, and re-layouts  7.06 us (3%)
  other arithmetic  3.6 us (1%)
    pallas_call x1, Pallas kernels, filtered_slab(): pl.pallas_call(field_kernel, out_shape=jax.ShapeDtypeStruct((CELLS, NORB)...  149 us
    pallas_call x1, Pallas kernels, sum_gram(): pl.pallas_call(functools.partial(sum_kernel, factor), out_shape=jax.Shape...  45.1 us
    pallas_call x1, Pallas kernels, rotate_home(): pl.pallas_call(home_kernel, out_shape=jax.ShapeDtypeStruct((4, ROWS, DEPT...  39.2 us
    pallas_call x1, Pallas kernels, inverse_factor(): pl.pallas_call(factor_kernel, out_shape=jax.ShapeDtypeStruct((size, size)...  24.6 us

profile of v3, /device:TPU:0, one launch (start us, length us, event | category | flops | bytes accessed | tf_op | source)
XLA Modules:
  0.0 268.9 jit_solution(10962874677789747325)
XLA Ops:
  0.6 0.7 broadcast_subtract_fusion
  1.3 0.1 pad.2.clone
  1.4 0.7 fusion.3
  2.0 0.7 fusion.4
  2.7 0.8 fusion.1
  3.5 0.1 eq.32
  3.6 0.1 copy.11
  3.7 0.1 compare_convert_fusion
  3.8 0.1 copy.12
  3.9 0.1 broadcast_multiply_fusion
  3.9 0.1 mul.51
  4.0 0.7 maximum_maximum_fusion.info
  4.7 2.1 reshape.98.proj
  6.8 148.6 %shard_map.77.part_ref.flat = f32[1536,512]{1,0:T(8,128)} custom-call(f32[4,32,48,128]{3,2,1,0:T(8,128)} %orb.1, f32[4,32,48]{2,1,0:T(8,128)} %pot.1, f32[32,4608]{1,0:T(8,128)} %reshape.98.proj, f32[32,128]{1,0:T(8,128)} %maximum_maximum_fusion.info), custom_call_target="tpu_custom_call" | custom-call | tf_op jit(solution)/shard_map/pallas_call | solution.py:679
  155.4 0.0 copy-start
  155.4 1.9 copy-done
  157.3 0.0 copy-start.1
  157.3 45.1 %shard_map.78.gram_ref = f32[512,512]{1,0:T(8,128)S(1)} custom-call(f32[1536,512]{1,0:T(8,128)S(1)} %copy-done), custom_call_target="tpu_custom_call" | custom-call | tf_op jit(solution)/shard_map/pallas_call | solution.py:265
  202.4 24.6 %shard_map.79.inverse = f32[512,512]{1,0:T(8,128)S(1)} custom-call(f32[512,512]{1,0:T(8,128)S(1)} %shard_map.78.gram_ref), custom_call_target="tpu_custom_call" | custom-call | tf_op jit(solution)/shard_map/pallas_call | solution.py:100
  227.0 0.0 copy-done.1
  227.1 39.2 %shard_map.80 = f32[4,32,48,128]{3,2,1,0:T(8,128)S(1)} custom-call(f32[1536,512]{1,0:T(8,128)S(1)} %copy-done.1, f32[512,512]{1,0:T(8,128)S(1)} %shard_map.79.inverse), custom_call_target="tpu_custom_call" | custom-call | tf_op jit(solution)/shard_map/pallas_call | solution.py:777
  266.2 1.7 copy.16
  267.9 1.0 copy.17
  (7 shorter events, 0.0 us)
Async XLA Ops:
  155.4 1.9 copy-start
  157.3 69.7 %copy-start.1 = (f32[1536,512]{1,0:T(8,128)S(1)}, f32[1536,512]{1,0:T(8,128)}, u32[]{:S(2)}) copy-start(f32[1536,512]{1,0:T(8,128)} %shard_map.77.part_ref.flat) | copy-start | bytes 9437188

commit v4 on v3

--- a/solution.py
+++ b/solution.py
@@ -294,6 +294,7 @@
 STRIPS = ROWS // STRIP
 PIECE = 4
 PIECES = ROWS // PIECE
+WINDOW = 3
 AREA = STRIP * DEPTH
 
 
@@ -308,7 +309,7 @@
 
 def field_kernel(
     orb, pot, proj, info, out,
-    e1, e2, second, shift_pot, nonlocal_plane, left, right, raw, notes, pot_all, corr, corr_in, weights,
+    e1, e2, second, shift_pot, nonlocal_plane, left, right, raw, notes, pot_all, corr_sum, corr, corr_in, weights,
     give_cross, give_keep, got_cross, got1, got2, slab,
     local_s, x_s, x_r, own_s, fwd_s, halo_r, small_s, small_r, core_s, core_r, next_s, next_r, last_s, last_r,
     corr_s, corr_r, y2_s, y2_r, out_s, out_r, self_s,
@@ -390,9 +391,6 @@
     pot_all[pl.ds(4 * half, 4)] = pot[...]
     for copy in loads:
         copy.wait()
-    pl.semaphore_wait(barrier, GROUP + 1)
-    for copy in small:
-        copy.start()
 
     def pack_piece(c, carry):
         for n in range(PIECE):
@@ -401,11 +399,19 @@
                 near, far = second[j, r], second[j + 2, r]
                 give_cross[j, r] = jnp.where(kept, swap(near), far)
                 give_keep[j, r] = jnp.where(kept, near, swap(far))
+        return carry
+
+    def start_piece(c):
         cross(c).start()
         keep(c).start()
-        return carry
-
-    lax.fori_loop(0, PIECES, pack_piece, 0)
+
+    lax.fori_loop(0, WINDOW, pack_piece, 0)
+    pl.semaphore_wait(barrier, GROUP + 1)
+    for copy in small:
+        copy.start()
+    for c in range(WINDOW):
+        start_piece(c)
+    lax.fori_loop(WINDOW, PIECES, pack_piece, 0)
 
     for copy in small_in:
         copy.wait_recv()
@@ -449,6 +455,10 @@
     def receive_piece(c):
         cross(c).wait_recv()
         forward(c).start()
+        cross(c).wait_send()
+        keep(c).wait_send()
+        if c + WINDOW < PIECES:
+            start_piece(c + WINDOW)
 
         def one(n, carry):
             r = c * PIECE + n
@@ -463,37 +473,21 @@
     for p in (2, 3):
         left[p, :, 128:256, :] = jnp.zeros((STRIPS, 128, AREA), jnp.bfloat16)
         right[p, :, 256:512] = jnp.zeros((CELLS, 256), jnp.bfloat16)
-    lax.fori_loop(0, 64, spread, 0)
-    across_in.wait_recv()
-    onward[1].start()
-    receive_piece(0)
-    store_pair(0, (1, 2), 0, 0)
-    store_pair(1, (1, 2), 1, 0)
-    receive_piece(1)
-    store_pair(2, (1, 2), 2, 0)
-    store_pair(3, (1, 2), 3, 0)
-    receive_piece(2)
-    for copy in onward:
-        copy.wait_recv()
-    last.start()
-    lax.fori_loop(64, 4 * ROWS, spread, 0)
-    receive_piece(3)
-    last_in.wait_recv()
-    store_pair(0, (0, 1), 4, 1)
-    store_pair(1, (0, 1), 5, 1)
-    for c in range(4, PIECES):
-        receive_piece(c)
-
-    def correlate(field, phase):
-        def part(n, total):
-            p, strip = n // STRIPS, lax.rem(n, STRIPS)
+    def spread_rows(n):
+        lax.fori_loop(n * 4 * ROWS // PIECES, (n + 1) * 4 * ROWS // PIECES, spread, 0)
+
+    def add_strip(field, strip):
+        def part(p, total):
             cells = field[4 + p, pl.ds(strip * STRIP, STRIP)].reshape(AREA, WIDE)
             both = jnp.concatenate(split(cells), axis=1)
             return total + lax.dot_general(
                 left[p, strip], both, (((1,), (0,)), ((), ())), preferred_element_type=jnp.float32)
 
-        total = lax.fori_loop(0, 4 * STRIPS, part, jnp.zeros((256, 2 * WIDE), jnp.float32))
-        total = total[:, :WIDE] + total[:, WIDE:]
+        corr_sum[...] = lax.fori_loop(0, 4, part, corr_sum[...])
+
+    def share_sums(phase):
+        total = corr_sum[:, :WIDE] + corr_sum[:, WIDE:]
+        corr_sum[...] = jnp.zeros_like(corr_sum)
         near, tail = total[0:64] + total[64:128], total[128:192] + total[192:256]
         corr[phase, 0] = tail[:PROJ]
         corr[phase, 1] = near[PROJ:]
@@ -561,41 +555,65 @@
 
         lax.fori_loop(0, 4, plane, 0)
 
-    copies1 = correlate(e1, 0)
-
-    def halo_strip(strip, carry):
+    def open_first(strip):
         for side in range(2):
             for n in range(STRIP // PIECE):
                 halo_in(side, strip * (STRIP // PIECE) + n).wait_recv()
         open_strip(e1, got1, strip)
-        return carry
-
-    lax.fori_loop(0, STRIPS, halo_strip, 0)
-
-    def sent_piece(c, carry):
-        cross(c).wait_send()
-        keep(c).wait_send()
+
+    spread_rows(0)
+    across_in.wait_recv()
+    onward[1].start()
+    receive_piece(0)
+    store_pair(0, (1, 2), 0, 0)
+    store_pair(1, (1, 2), 1, 0)
+    spread_rows(1)
+    receive_piece(1)
+    store_pair(2, (1, 2), 2, 0)
+    store_pair(3, (1, 2), 3, 0)
+    spread_rows(2)
+    receive_piece(2)
+    for copy in onward:
+        copy.wait_recv()
+    last.start()
+    spread_rows(3)
+    spread_rows(4)
+    receive_piece(3)
+    last_in.wait_recv()
+    store_pair(0, (0, 1), 4, 1)
+    store_pair(1, (0, 1), 5, 1)
+    corr_sum[...] = jnp.zeros_like(corr_sum)
+    add_strip(e1, 0)
+    receive_piece(4)
+    spread_rows(5)
+    add_strip(e1, 1)
+    receive_piece(5)
+    spread_rows(6)
+    open_first(0)
+    receive_piece(6)
+    spread_rows(7)
+    add_strip(e1, 2)
+    receive_piece(7)
+    add_strip(e1, 3)
+    copies1 = share_sums(0)
+    for strip in range(1, STRIPS):
+        open_first(strip)
+    for c in range(PIECES):
         forward(c).wait_send()
-        return carry
-
-    lax.fori_loop(0, PIECES, sent_piece, 0)
     weigh(0, copies1)
 
     def write_first(p, r, value):
         e2[p + 4, r] = value
 
-    def strip_rows(strip):
-        return pl.ds(strip * STRIP, STRIP)
-
-    def up2(strip):
-        at = strip_rows(strip)
-        return send(give_cross.at[:, at], got2.at[0, :, at], y2_s.at[0, strip], y2_r.at[0, strip], at_pair(1))
-
-    def down2(strip):
-        at = strip_rows(strip)
-        return send(give_keep.at[:, at], got2.at[1, :, at], y2_s.at[1, strip], y2_r.at[1, strip], at_pair(-1))
-
-    def first_strip(strip, carry):
+    def up2(c):
+        at = piece_rows(c)
+        return send(give_cross.at[:, at], got2.at[0, :, at], y2_s.at[0, c], y2_r.at[0, c], at_pair(1))
+
+    def down2(c):
+        at = piece_rows(c)
+        return send(give_keep.at[:, at], got2.at[1, :, at], y2_s.at[1, c], y2_r.at[1, c], at_pair(-1))
+
+    def first_strip(strip):
         apply(e1, strip, 1.0 / 6.0, write_first)
 
         def pack(n, inner):
@@ -607,12 +625,15 @@
             return inner
 
         lax.fori_loop(0, STRIP, pack, 0)
-        up2(strip).start()
-        down2(strip).start()
-        return carry
-
-    lax.fori_loop(0, STRIPS, first_strip, 0)
-    copies2 = correlate(e2, 1)
+        for c in range(2 * strip, 2 * strip + 2):
+            if c < WINDOW:
+                up2(c).start()
+                down2(c).start()
+        add_strip(e2, strip)
+
+    for strip in range(STRIPS):
+        first_strip(strip)
+    copies2 = share_sums(1)
     weigh(1, copies2)
 
     def write_second(p, r, value):
@@ -627,19 +648,24 @@
         src = second.at[rank // 2, pl.ds(lax.rem(rank, 2) * 16 + part * STRIP, STRIP)]
         return pltpu.make_async_copy(src, slab.at[rank, pl.ds(part * STRIP, STRIP)], self_s.at[part])
 
-    def second_strip(strip, carry):
-        up2(strip).wait_recv()
-        down2(strip).wait_recv()
+    def second_strip(strip):
+        for c in range(2 * strip, 2 * strip + 2):
+            for copy in (up2(c), down2(c)):
+                copy.wait_recv()
+                copy.wait_send()
+            if c + WINDOW < PIECES:
+                up2(c + WINDOW).start()
+                down2(c + WINDOW).start()
         open_strip(e2, got2, strip)
         apply(e2, strip, 1.0 / 3.0, write_second)
-        part = lax.rem(strip, 2)
+        part = strip % 2
         for n in range(4):
             index = 2 * lax.rem(n + rank // 2 + 2, 4) + strip // 2
             pl.when(index != rank)(lambda index=index: give(index, part).start())
         pl.when(lax.rem(rank, 2) == strip // 2)(own_part(part).start)
-        return carry
-
-    lax.fori_loop(0, STRIPS, second_strip, 0)
+
+    for strip in range(STRIPS):
+        second_strip(strip)
 
     for n in range(1, GROUP):
         index = lax.rem(rank + n, GROUP)
@@ -663,9 +689,6 @@
 
     for copy in small + [across, last] + onward + copies1 + copies2:
         copy.wait_send()
-    for strip in range(STRIPS):
-        up2(strip).wait_send()
-        down2(strip).wait_send()
     for n in range(1, GROUP):
         for part in range(2):
             give(lax.rem(rank + n, GROUP), part).wait_send()
@@ -692,6 +715,7 @@
             pltpu.VMEM((3, PROJ, SPAN * CELLS), f32),
             pltpu.VMEM((3, PROJ, 128), f32),
             pltpu.VMEM((8, ROWS, DEPTH), f32),
+            pltpu.VMEM((256, 2 * WIDE), f32),
             pltpu.VMEM((2, 3, PROJ, WIDE), f32),
             pltpu.VMEM((2, 2, PROJ, WIDE), f32),
             pltpu.VMEM((512, WIDE), bf16),
@@ -703,7 +727,7 @@
             pltpu.VMEM((GROUP, ROWS // 2, DEPTH, WIDE), f32),
             dma((4,)), dma((PIECES,)), dma((PIECES,)), dma((PIECES,)), dma((PIECES,)), dma((2, PIECES)),
             dma((3,)), dma((3,)), dma(()), dma(()), dma((2,)), dma((2,)), dma(()), dma(()),
-            dma((2, 2)), dma((2, 2)), dma((2, STRIPS)), dma((2, STRIPS)),
+            dma((2, 2)), dma((2, 2)), dma((2, PIECES)), dma((2, PIECES)),
             dma((GROUP, 2)), dma((GROUP, 2)), dma((2,)),
         ],
         compiler_params=pltpu.CompilerParams(collective_id=2, has_side_effects=True, vmem_limit_bytes=62 * 2**20),

time: 270 us -> 233 us (0.86)
  Pallas kernels: 257 us -> 221 us
    pallas_call x1, Pallas kernels: 149 us -> 123 us  [filtered_slab(): pl.pallas_call(field_kernel, out_shape=jax.ShapeDtypeStruct((CELLS, NORB)...]
    pallas_call x1, Pallas kernels: 45.1 us -> 33.8 us  [sum_gram(): pl.pallas_call(functools.partial(sum_kernel, factor), out_shape=jax.Shape...]
where the time goes in v4:
time: 233 us; the launch traced here: 232 us
  Pallas kernels  221 us (95%)
  local copies, waits for them, and re-layouts  7.06 us (3%)
  other arithmetic  3.6 us (2%)
    pallas_call x1, Pallas kernels, filtered_slab(): pl.pallas_call(field_kernel, out_shape=jax.ShapeDtypeStruct((CELLS, NORB)...  123 us
    pallas_call x1, Pallas kernels, rotate_home(): pl.pallas_call(home_kernel, out_shape=jax.ShapeDtypeStruct((4, ROWS, DEPT...  39 us
    pallas_call x1, Pallas kernels, sum_gram(): pl.pallas_call(functools.partial(sum_kernel, factor), out_shape=jax.Shape...  33.8 us
    pallas_call x1, Pallas kernels, inverse_factor(): pl.pallas_call(factor_kernel, out_shape=jax.ShapeDtypeStruct((size, size)...  24.6 us

profile of v4, /device:TPU:0, one launch (start us, length us, event | category | flops | bytes accessed | tf_op | source)
XLA Modules:
  0.0 232.1 jit_solution(11467054734117282262)
XLA Ops:
  0.6 0.7 broadcast_subtract_fusion
  1.3 0.1 pad.2.clone
  1.4 0.7 fusion.3
  2.0 0.7 fusion.4
  2.7 0.8 fusion.1
  3.5 0.1 eq.32
  3.6 0.1 copy.11
  3.7 0.1 compare_convert_fusion
  3.8 0.1 copy.12
  3.9 0.1 broadcast_multiply_fusion
  3.9 0.1 mul.51
  4.0 0.7 maximum_maximum_fusion.info
  4.7 2.1 reshape.98.proj
  6.8 123.2 %shard_map.77.part_ref.flat = f32[1536,512]{1,0:T(8,128)} custom-call(f32[4,32,48,128]{3,2,1,0:T(8,128)} %orb.1, f32[4,32,48]{2,1,0:T(8,128)} %pot.1, f32[32,4608]{1,0:T(8,128)} %reshape.98.proj, f32[32,128]{1,0:T(8,128)} %maximum_maximum_fusion.info), custom_call_target="tpu_custom_call" | custom-call | tf_op jit(solution)/shard_map/pallas_call | solution.py:702
  130.0 0.0 copy-start
  130.1 1.9 copy-done
  131.9 0.0 copy-start.1
  131.9 33.8 %shard_map.78.gram_ref = f32[512,512]{1,0:T(8,128)S(1)} custom-call(f32[1536,512]{1,0:T(8,128)S(1)} %copy-done), custom_call_target="tpu_custom_call" | custom-call | tf_op jit(solution)/shard_map/pallas_call | solution.py:265
  165.8 24.6 %shard_map.79.inverse = f32[512,512]{1,0:T(8,128)S(1)} custom-call(f32[512,512]{1,0:T(8,128)S(1)} %shard_map.78.gram_ref), custom_call_target="tpu_custom_call" | custom-call | tf_op jit(solution)/shard_map/pallas_call | solution.py:100
  190.4 0.0 copy-done.1
  190.4 39.0 %shard_map.80 = f32[4,32,48,128]{3,2,1,0:T(8,128)S(1)} custom-call(f32[1536,512]{1,0:T(8,128)S(1)} %copy-done.1, f32[512,512]{1,0:T(8,128)S(1)} %shard_map.79.inverse), custom_call_target="tpu_custom_call" | custom-call | tf_op jit(solution)/shard_map/pallas_call | solution.py:801
  229.4 1.7 copy.16
  231.1 1.0 copy.17
  (7 shorter events, 0.0 us)
Async XLA Ops:
  130.0 1.9 copy-start
  131.9 58.5 %copy-start.1 = (f32[1536,512]{1,0:T(8,128)S(1)}, f32[1536,512]{1,0:T(8,128)}, u32[]{:S(2)}) copy-start(f32[1536,512]{1,0:T(8,128)} %shard_map.77.part_ref.flat) | copy-start | bytes 9437188

commit v5 on v4

--- a/solution.py
+++ b/solution.py
@@ -69,9 +69,8 @@
     return done
 
 
-def factor_kernel(gram_ref, inverse_ref, work):
+def factor_steps(work, done):
     size = work.shape[0]
-    work[...] = gram_ref[...]
 
     def step(k, carry):
         at = pl.ds(pl.multiple_of(k * B, B), B)
@@ -81,30 +80,16 @@
         column = jnp.where(row_id >= (k + 1) * B, work[:, at], 0.0)
         unit = lax.broadcasted_iota(jnp.int32, (B, B), 0) == lax.broadcasted_iota(jnp.int32, (B, B), 1)
         work[at, at] = jnp.where(unit, 1.0, 0.0)
+        scaled = dot_f32(corner, work[at, :], ((1,), (0,)))
+        row_at = lax.broadcasted_iota(jnp.int32, (B, size), 0) + k * B
+        done(k, jnp.where(lax.broadcasted_iota(jnp.int32, (B, size), 1) <= row_at, scaled, 0.0))
         below = dot_f32(column, corner, ((1,), (1,)))
-        scaled = dot_f32(corner, work[at, :], ((1,), (0,)))
         block = work[:, at]
         work[:, at] = jnp.where(row_id >= (k + 1) * B, 0.0, block)
         work[...] = work[...] - dot_f32(below, scaled, ((1,), (0,)))
-        work[at, :] = scaled
         return carry
 
     lax.fori_loop(0, size // B, step, 0)
-    row_id = lax.broadcasted_iota(jnp.int32, (size, size), 0)
-    col_id = lax.broadcasted_iota(jnp.int32, (size, size), 1)
-    inverse_ref[...] = jnp.where(col_id <= row_id, work[...], 0.0)
-
-
-def inverse_factor(gram):
-    size = gram.shape[0]
-    return pl.pallas_call(
-        factor_kernel,
-        out_shape=jax.ShapeDtypeStruct((size, size), jnp.float32),
-        in_specs=[pl.BlockSpec(memory_space=pltpu.VMEM)],
-        out_specs=pl.BlockSpec(memory_space=pltpu.VMEM),
-        scratch_shapes=[pltpu.VMEM((size, size), jnp.float32)],
-        compiler_params=pltpu.CompilerParams(vmem_limit_bytes=32 * 2**20),
-    )(gram)
 
 
 MESH = pl.DeviceIdType.MESH
@@ -117,12 +102,15 @@
     return [(i, j) for i in range(size // B) for j in range(i + 1)]
 
 
-def sum_kernel(factor, part_ref, gram_ref, high, low, pack, near, mine, far, total, near_s, near_r, far_s, far_r, out_s, out_r, end_s, end_r):
+def finish_part(
+    factor, gram_ref, filtered_ref,
+    high, low, pack, near, mine, far, total, work, parts, near_s, near_r, far_s, far_r, out_s, out_r, end_s, end_r,
+    local_s, home_s, home_r,
+):
     band, dom = lax.axis_index("band"), lax.axis_index("dom")
     pair, half = dom // 2, dom % 2
     rank = half * 4 + band
-    size = part_ref.shape[1]
-    blocks = tri_blocks(size)
+    blocks = tri_blocks(work.shape[0])
     share = len(blocks) * B // NEAR
     piece = share // SUMMERS
 
@@ -133,29 +121,6 @@
     def far_peer(step):
         other = (pair + step) % FAR
         return other, (band, other * 2 + half)
-
-    barrier = pltpu.get_barrier_semaphore()
-    for step in range(1, NEAR):
-        pl.semaphore_signal(barrier, inc=1, device_id=near_peer(step)[1], device_id_type=MESH)
-    for step in range(1, FAR):
-        pl.semaphore_signal(barrier, inc=1, device_id=far_peer(step)[1], device_id_type=MESH)
-    contract = (((0,), (0,)), ((), ()))
-
-    def split_rows(n, carry):
-        at = pl.ds(pl.multiple_of(n * 128, 128), 128)
-        high[at, :], low[at, :] = split(part_ref[at, :])
-        return carry
-
-    lax.fori_loop(0, part_ref.shape[0] // 128, split_rows, 0)
-    for i in range(size // B):
-        own, wide = slice(i * B, (i + 1) * B), slice(0, (i + 1) * B)
-        block_row = lax.dot_general(high[:, own], high[:, wide], contract, preferred_element_type=jnp.float32)
-        block_row += lax.dot_general(high[:, own], low[:, wide], contract, preferred_element_type=jnp.float32)
-        block_row += lax.dot_general(low[:, own], high[:, wide], contract, preferred_element_type=jnp.float32)
-        for j in range(i + 1):
-            n = blocks.index((i, j))
-            pack[n * B : (n + 1) * B, :] = block_row[:, j * B : (j + 1) * B]
-    pl.semaphore_wait(barrier, NEAR + FAR - 2)
 
     def rows(index, count):
         return pl.ds(pl.multiple_of(index * count, 8), count)
@@ -243,6 +208,44 @@
         gram_ref[i * B : (i + 1) * B, j * B : (j + 1) * B] = block
         if i != j:
             gram_ref[j * B : (j + 1) * B, i * B : (i + 1) * B] = block.T
+    work[...] = gram_ref[...]
+
+    def target(index):
+        return filtered_ref.at[index // 2, pl.ds(pl.multiple_of(lax.rem(index, 2) * 16, 8), ROWS // 2)]
+
+    def move(k, to_half):
+        return pltpu.make_async_remote_copy(
+            src_ref=parts.at[k, rows(to_half, ROWS // 2)], dst_ref=target(rank), send_sem=home_s.at[k, to_half],
+            recv_sem=home_r.at[rank], device_id=(k, pair * 2 + to_half), device_id_type=MESH)
+
+    local = pltpu.make_async_copy(parts.at[band, rows(half, ROWS // 2)], target(rank), local_s)
+    across = (((1,), (1,)), ((), ()))
+    cells = high.shape[0] // 2
+
+    def rotate(k, inverse_rows):
+        high_rot, low_rot = split(inverse_rows)
+        both = jnp.concatenate([high_rot, low_rot], axis=0)
+        for to_half in range(2):
+            at = slice(to_half * cells, (to_half + 1) * cells)
+            wide = lax.dot_general(high[at, :], both, across, preferred_element_type=jnp.float32)
+            more = lax.dot_general(low[at, :], high_rot, across, preferred_element_type=jnp.float32)
+            value = wide[:, :B] + (wide[:, B:] + more)
+            parts[k, rows(to_half, ROWS // 2)] = value.reshape(ROWS // 2, DEPTH, B)
+            here = (k == band) & (to_half == half)
+            pl.when(jnp.logical_not(here))(lambda to_half=to_half: move(k, to_half).start())
+            pl.when(here)(local.start)
+
+    factor_steps(work, rotate)
+    for step in range(1, NEAR):
+        other, device = near_peer(step)
+        pltpu.make_async_remote_copy(
+            src_ref=parts.at[0, rows(0, ROWS // 2)], dst_ref=target(other), send_sem=home_s.at[0, 0], recv_sem=home_r.at[other],
+            device_id=device, device_id_type=MESH).wait_recv()
+    local.wait()
+    for k in range(4):
+        for to_half in range(2):
+            here = (k == band) & (to_half == half)
+            pl.when(jnp.logical_not(here))(lambda k=k, to_half=to_half: move(k, to_half).wait_send())
 
     for step in range(1, NEAR):
         near_copy(step).wait_send()
@@ -255,31 +258,6 @@
     def _():
         for step in range(1, FAR):
             out_copy(step).wait_send()
-
-
-def sum_gram(part, factor):
-    cells, size = part.shape
-    packed = len(tri_blocks(size)) * B
-    share = packed // NEAR
-    dma = pltpu.SemaphoreType.DMA
-    return pl.pallas_call(
-        functools.partial(sum_kernel, factor),
-        out_shape=jax.ShapeDtypeStruct((size, size), jnp.float32),
-        in_specs=[pl.BlockSpec(memory_space=pltpu.VMEM)],
-        out_specs=pl.BlockSpec(memory_space=pltpu.VMEM),
-        scratch_shapes=[
-            pltpu.VMEM((cells, size), jnp.bfloat16),
-            pltpu.VMEM((cells, size), jnp.bfloat16),
-            pltpu.VMEM((packed, B), jnp.float32),
-            pltpu.VMEM((NEAR, share, B), jnp.float32),
-            pltpu.VMEM((share, B), jnp.float32),
-            pltpu.VMEM((FAR, share // SUMMERS, B), jnp.float32),
-            pltpu.VMEM((packed, B), jnp.float32),
-            dma((NEAR,)), dma((NEAR,)), dma((FAR,)), dma((FAR,)),
-            dma((FAR,)), dma((FAR,)), dma((NEAR,)), dma((NEAR,)),
-        ],
-        compiler_params=pltpu.CompilerParams(collective_id=1, has_side_effects=True, vmem_limit_bytes=32 * 2**20),
-    )(part)
 
 
 ROWS = 32
@@ -307,12 +285,13 @@
     return pltpu.roll(value, WIDE // 2, value.ndim - 1)
 
 
-def field_kernel(
-    orb, pot, proj, info, out,
+def whole_kernel(
+    factor, orb, pot, proj, info, gram_ref, filtered_ref,
     e1, e2, second, shift_pot, nonlocal_plane, left, right, raw, notes, pot_all, corr_sum, corr, corr_in, weights,
     give_cross, give_keep, got_cross, got1, got2, slab,
     local_s, x_s, x_r, own_s, fwd_s, halo_r, small_s, small_r, core_s, core_r, next_s, next_r, last_s, last_r,
     corr_s, corr_r, y2_s, y2_r, out_s, out_r, self_s,
+    high_cells, low_cells, pack, *rest,
 ):
     band, dom = lax.axis_index("band"), lax.axis_index("dom")
     pair, half = dom // 2, dom % 2
@@ -334,8 +313,10 @@
         return (lax.rem(index, 4), pair * 2 + index // 4)
 
     barrier = pltpu.get_barrier_semaphore()
-    for peer in [at_pair(1), at_pair(-1)] + [member(lax.rem(rank + n, GROUP)) for n in range(1, GROUP)]:
-        pl.semaphore_signal(barrier, inc=1, device_id=peer, device_id_type=MESH)
+    for n in range(1, GROUP):
+        pl.semaphore_signal(barrier, inc=1, device_id=member(lax.rem(rank + n, GROUP)), device_id_type=MESH)
+    for n in range(1, FAR):
+        pl.semaphore_signal(barrier, inc=1, device_id=at_pair(n), device_id_type=MESH)
 
     loads = [pltpu.make_async_copy(orb.at[p], second.at[p], local_s.at[p]) for p in range(4)]
     for copy in loads:
@@ -349,12 +330,12 @@
     small = [
         send(pot, pot_all.at[pl.ds(4 * half, 4)], small_s.at[0], small_r.at[0], partner),
         send(info, notes.at[1 + half], small_s.at[1], small_r.at[1], partner),
-        send(proj.at[share], raw.at[1 + half, share], small_s.at[2], small_r.at[2], partner),
+        send(raw.at[1 + half, share], raw.at[1 + half, share], small_s.at[2], small_r.at[2], partner),
     ]
     small_in = [
         send(pot, pot_all.at[pl.ds(4 * other, 4)], small_s.at[0], small_r.at[0], partner),
         send(info, notes.at[1 + other], small_s.at[1], small_r.at[1], partner),
-        send(proj.at[share], raw.at[1 + other, share], small_s.at[2], small_r.at[2], partner),
+        send(raw.at[1 + other, share], raw.at[1 + other, share], small_s.at[2], small_r.at[2], partner),
     ]
     across = send(raw.at[1 + other, share], raw.at[1 + other, share], core_s, core_r, sibling)
     across_in = send(raw.at[1 + other, twin], raw.at[1 + other, twin], core_s, core_r, sibling)
@@ -387,7 +368,8 @@
         return send(give_keep.at[:, at], got1.at[side, :, at], own_s.at[c], halo_r.at[side, c], at_pair(1))
 
     notes[1 + half] = info[...]
-    raw[1 + half] = proj[...]
+    for a in range(PROJ // MAXPROJ):
+        raw[1 + half, a * MAXPROJ : (a + 1) * MAXPROJ, :] = proj[a]
     pot_all[pl.ds(4 * half, 4)] = pot[...]
     for copy in loads:
         copy.wait()
@@ -406,7 +388,7 @@
         keep(c).start()
 
     lax.fori_loop(0, WINDOW, pack_piece, 0)
-    pl.semaphore_wait(barrier, GROUP + 1)
+    pl.semaphore_wait(barrier, GROUP + FAR - 2)
     for copy in small:
         copy.start()
     for c in range(WINDOW):
@@ -667,43 +649,68 @@
     for strip in range(STRIPS):
         second_strip(strip)
 
-    for n in range(1, GROUP):
-        index = lax.rem(rank + n, GROUP)
-        for part in range(2):
-            send(second.at[0, pl.ds(0, STRIP)], slab.at[index, pl.ds(part * STRIP, STRIP)], out_s.at[index, part],
-                 out_r.at[index, part], member(index)).wait_recv()
-    own_part(0).wait()
-    own_part(1).wait()
+    blocks = tri_blocks(NORB)
+    pack[...] = jnp.zeros_like(pack)
 
     def repack(n, carry):
-        cells = pl.ds(pl.multiple_of(n * DEPTH, 8), DEPTH)
-        more = pl.ds(pl.multiple_of(CELLS // 2 + n * DEPTH, 8), DEPTH)
+        cells = pl.ds(pl.multiple_of(n * DEPTH, 16), DEPTH)
+        more = pl.ds(pl.multiple_of(CELLS // 2 + n * DEPTH, 16), DEPTH)
         for b in range(4):
             at = slice(b * WIDE, (b + 1) * WIDE)
             here, there = slab[b, n], slab[4 + b, n]
-            out[cells, at] = jnp.where(lower, here, swap(there))
-            out[more, at] = jnp.where(lower, swap(here), there)
+            high_cells[cells, at], low_cells[cells, at] = split(jnp.where(lower, here, swap(there)))
+            high_cells[more, at], low_cells[more, at] = split(jnp.where(lower, swap(here), there))
         return carry
 
-    lax.fori_loop(0, ROWS // 2, repack, 0)
+    def add_gram(part):
+        contract = (((0,), (0,)), ((), ()))
+
+        def chunk(side, carry):
+            cells = pl.ds(pl.multiple_of(side * (CELLS // 2) + part * AREA, 16), AREA)
+            for i in range(NORB // B):
+                own, wide = slice(i * B, (i + 1) * B), slice(0, (i + 1) * B)
+                row = lax.dot_general(
+                    high_cells[cells, own], high_cells[cells, wide], contract, preferred_element_type=jnp.float32)
+                row += lax.dot_general(
+                    high_cells[cells, own], low_cells[cells, wide], contract, preferred_element_type=jnp.float32)
+                row += lax.dot_general(
+                    low_cells[cells, own], high_cells[cells, wide], contract, preferred_element_type=jnp.float32)
+                for j in range(i + 1):
+                    n = blocks.index((i, j))
+                    pack[n * B : (n + 1) * B, :] += row[:, j * B : (j + 1) * B]
+            return carry
+
+        lax.fori_loop(0, 2, chunk, 0)
+
+    for part in range(2):
+        for n in range(1, GROUP):
+            index = lax.rem(rank + n, GROUP)
+            send(second.at[0, pl.ds(0, STRIP)], slab.at[index, pl.ds(part * STRIP, STRIP)], out_s.at[index, part],
+                 out_r.at[index, part], member(index)).wait_recv()
+        own_part(part).wait()
+        lax.fori_loop(part * STRIP, (part + 1) * STRIP, repack, 0)
+        add_gram(part)
 
     for copy in small + [across, last] + onward + copies1 + copies2:
         copy.wait_send()
     for n in range(1, GROUP):
         for part in range(2):
             give(lax.rem(rank + n, GROUP), part).wait_send()
-
-
-def filtered_slab(orbitals, potential, projectors, info):
+    finish_part(factor, gram_ref, filtered_ref, high_cells, low_cells, pack, *rest[:5], second, *rest[5:])
+
+
+def run(orbitals, potential, projectors, info, factor):
     dma = pltpu.SemaphoreType.DMA
     f32, bf16 = jnp.float32, jnp.bfloat16
-    vmem = pl.BlockSpec(memory_space=pltpu.VMEM)
+    vmem, hbm = pl.BlockSpec(memory_space=pltpu.VMEM), pl.BlockSpec(memory_space=pl.ANY)
     block = (ROWS, DEPTH, WIDE)
+    packed = len(tri_blocks(NORB)) * B
+    share = packed // NEAR
     return pl.pallas_call(
-        field_kernel,
-        out_shape=jax.ShapeDtypeStruct((CELLS, NORB), f32),
-        in_specs=[pl.BlockSpec(memory_space=pl.ANY), vmem, vmem, vmem],
-        out_specs=vmem,
+        functools.partial(whole_kernel, factor),
+        out_shape=[jax.ShapeDtypeStruct((NORB, NORB), f32), jax.ShapeDtypeStruct((4,) + block, f32)],
+        in_specs=[hbm, vmem, vmem, vmem],
+        out_specs=[vmem, hbm],
         scratch_shapes=[
             pltpu.VMEM((12,) + block, f32),
             pltpu.VMEM((12,) + block, f32),
@@ -729,87 +736,20 @@
             dma((3,)), dma((3,)), dma(()), dma(()), dma((2,)), dma((2,)), dma(()), dma(()),
             dma((2, 2)), dma((2, 2)), dma((2, PIECES)), dma((2, PIECES)),
             dma((GROUP, 2)), dma((GROUP, 2)), dma((2,)),
+            pltpu.VMEM((CELLS, NORB), bf16),
+            pltpu.VMEM((CELLS, NORB), bf16),
+            pltpu.VMEM((packed, B), f32),
+            pltpu.VMEM((NEAR, share, B), f32),
+            pltpu.VMEM((share, B), f32),
+            pltpu.VMEM((FAR, share // SUMMERS, B), f32),
+            pltpu.VMEM((packed, B), f32),
+            pltpu.VMEM((NORB, NORB), f32),
+            dma((NEAR,)), dma((NEAR,)), dma((FAR,)), dma((FAR,)),
+            dma((FAR,)), dma((FAR,)), dma((NEAR,)), dma((NEAR,)),
+            dma(()), dma((4, 2)), dma((NEAR,)),
         ],
         compiler_params=pltpu.CompilerParams(collective_id=2, has_side_effects=True, vmem_limit_bytes=62 * 2**20),
     )(orbitals, potential, projectors, info)
-
-
-def home_kernel(flat, inverse, out, parts, turned, local_s, send_s, recv_s):
-    band, dom = lax.axis_index("band"), lax.axis_index("dom")
-    pair, half = dom // 2, dom % 2
-    rank = half * 4 + band
-    place, core = (band // 2) * 2 + half, lax.rem(band, 2)
-    barrier = pltpu.get_barrier_semaphore()
-    for step in range(1, GROUP):
-        index = lax.rem(rank + step, GROUP)
-        pl.semaphore_signal(
-            barrier, inc=1, device_id=(lax.rem(index, 4), pair * 2 + index // 4), device_id_type=MESH)
-    high_part, low_part = split(inverse[...])
-    turned[0], turned[1] = high_part, low_part
-
-    def target(index):
-        return out.at[index // 2, pl.ds(pl.multiple_of(lax.rem(index, 2) * 16, 8), ROWS // 2)]
-
-    def choice(n):
-        chip = lax.rem(place + (2, 1, 3, 0)[n // 2], 4)
-        return lax.rem(chip, 2), (chip // 2) * 2 + lax.rem(core + 1 + n, 2)
-
-    def move(n):
-        to_half, to_band = choice(n)
-        return pltpu.make_async_remote_copy(
-            src_ref=parts.at[n], dst_ref=target(rank), send_sem=send_s.at[n], recv_sem=recv_s.at[rank],
-            device_id=(to_band, pair * 2 + to_half), device_id_type=MESH)
-
-    local = pltpu.make_async_copy(parts.at[GROUP - 1], target(rank), local_s)
-    contract = (((1,), (1,)), ((), ()))
-    for n in range(GROUP):
-        to_half, to_band = choice(n)
-        rows = pl.ds(pl.multiple_of(to_band * B, B), B)
-
-        def tile(m, carry, n=n, to_half=to_half, rows=rows):
-            size = CELLS // 8
-            cells = flat[pl.ds(pl.multiple_of(to_half * (CELLS // 2) + m * size, 8), size), :]
-            high_cells, low_cells = split(cells)
-            high_rot, low_rot = turned[0, rows, :], turned[1, rows, :]
-            both = jnp.concatenate([high_rot, low_rot], axis=0)
-            wide = lax.dot_general(high_cells, both, contract, preferred_element_type=jnp.float32)
-            more = lax.dot_general(low_cells, high_rot, contract, preferred_element_type=jnp.float32)
-            value = wide[:, :B] + (wide[:, B:] + more)
-            parts[n, pl.ds(m * (size // DEPTH), size // DEPTH)] = value.reshape(size // DEPTH, DEPTH, WIDE)
-            return carry
-
-        lax.fori_loop(0, 4, tile, 0)
-        if n == 0:
-            pl.semaphore_wait(barrier, GROUP - 1)
-        if n < GROUP - 1:
-            move(n).start()
-        else:
-            local.start()
-    for step in range(1, GROUP):
-        index = lax.rem(rank + step, GROUP)
-        pltpu.make_async_remote_copy(
-            src_ref=parts.at[0], dst_ref=target(index), send_sem=send_s.at[0], recv_sem=recv_s.at[index],
-            device_id=(lax.rem(index, 4), pair * 2 + index // 4), device_id_type=MESH).wait_recv()
-    local.wait()
-    for n in range(GROUP - 1):
-        move(n).wait_send()
-
-
-def rotate_home(flat, inverse):
-    dma = pltpu.SemaphoreType.DMA
-    vmem = pl.BlockSpec(memory_space=pltpu.VMEM)
-    return pl.pallas_call(
-        home_kernel,
-        out_shape=jax.ShapeDtypeStruct((4, ROWS, DEPTH, WIDE), jnp.float32),
-        in_specs=[vmem, vmem],
-        out_specs=pl.BlockSpec(memory_space=pl.ANY),
-        scratch_shapes=[
-            pltpu.VMEM((GROUP, ROWS // 2, DEPTH, WIDE), jnp.float32),
-            pltpu.VMEM((2, NORB, NORB), jnp.bfloat16),
-            dma(()), dma((GROUP,)), dma((GROUP,)),
-        ],
-        compiler_params=pltpu.CompilerParams(collective_id=3, has_side_effects=True, vmem_limit_bytes=40 * 2**20),
-    )(flat, inverse)
 
 
 def shards(orbitals, potential, projectors, coupling, atom_plane, projector_count):
@@ -830,10 +770,8 @@
     blocks = (sym_coupling[:, :, None, :] * same_atom[:, None, :, None]).reshape(PROJ, PROJ)
     info = jnp.concatenate(
         [blocks, flags, jnp.zeros((PROJ, 128 - PROJ - REACH * SPAN), jnp.float32)], axis=1)
-    flat = filtered_slab(orbitals, potential, projectors.reshape(PROJ, SPAN * CELLS), info)
     total_cells = planes * side_y * side_z * lax.axis_size("dom")
-    gram = sum_gram(flat, 1.0 / total_cells)
-    filtered = rotate_home(flat, inverse_factor(gram))
+    gram, filtered = run(orbitals, potential, projectors, info, 1.0 / total_cells)
     return (filtered, gram)
 
 

time: 233 us -> 220 us (0.944)
  Pallas kernels: 221 us -> 209 us
    pallas_call x4 -> x1, Pallas kernels: 221 us -> 209 us  [run(): pl.pallas_call(functools.partial(whole_kernel, factor), out_shape=[jax.Sh...]
    unnamed x6 -> x4, local copies, waits for them, and re-layouts: 4.52 us -> 4.93 us
where the time goes in v5:
time: 220 us; the launch traced here: 219 us
  Pallas kernels  209 us (95%)
  local copies, waits for them, and re-layouts  5.4 us (2%)
  other arithmetic  3.6 us (2%)
    pallas_call x1, Pallas kernels, run(): pl.pallas_call(functools.partial(whole_kernel, factor), out_shape=[jax.Sh...  209 us
    unnamed x4, local copies, waits for them, and re-layouts  4.93 us

profile of v5, /device:TPU:0, one launch (start us, length us, event | category | flops | bytes accessed | tf_op | source)
XLA Modules:
  0.0 218.7 jit_solution(10445924120752322948)
XLA Ops:
  0.6 0.7 broadcast_subtract_fusion
  1.3 0.1 pad.2.clone
  1.4 0.7 fusion.3
  2.0 0.7 fusion.4
  2.7 0.8 fusion.1
  3.5 0.1 eq.32
  3.6 0.1 copy.11
  3.7 0.1 compare_convert_fusion
  3.8 0.1 copy.12
  3.9 0.1 broadcast_multiply_fusion
  3.9 0.1 mul.51
  4.0 0.7 maximum_maximum_fusion.info
  4.7 209.0 %shard_map.77 = (f32[512,512]{1,0:T(8,128)}, f32[4,32,48,128]{3,2,1,0:T(8,128)}) custom-call(f32[4,32,48,128]{3,2,1,0:T(8,128)} %orb.1, f32[4,32,48]{2,1,0:T(8,128)} %pot.1, f32[8,4,4608]{2,1,0:T(4,128)} %proj.1, f32[32,128]{1,0:T(8,128)} %maximum_maximum_fusion.info), custom_call_target="tpu_custom_call" | custom-call | tf_op jit(solution)/shard_map/pallas_call | solution.py:709
  213.8 0.0 copy-start
  213.8 4.0 %copy.16 = f32[4,32,48,128]{3,2,1,0:T(8,128)} copy(f32[4,32,48,128]{3,2,1,0:T(8,128)} %get-tuple-element.8) | data formatting | bytes 6291456
  217.8 0.0 copy-done
  217.8 1.0 copy.17
  (7 shorter events, 0.0 us)
Async XLA Ops:
  213.8 4.0 %copy-start = (f32[512,512]{1,0:T(8,128)S(1)}, f32[512,512]{1,0:T(8,128)}, u32[]{:S(2)}) copy-start(f32[512,512]{1,0:T(8,128)} %get-tuple-element.9) | copy-start | bytes 3145732

commit v6 on v5

--- a/solution.py
+++ b/solution.py
@@ -69,13 +69,15 @@
     return done
 
 
-def factor_steps(work, done):
+def factor_steps(work, begin, complete, done):
     size = work.shape[0]
 
     def step(k, carry):
         at = pl.ds(pl.multiple_of(k * B, B), B)
+        pl.when(k == 0)(begin)
         tiles = [work[pl.ds(pl.multiple_of(k * B + 8 * t, 8), 8), at] for t in range(B // 8)]
         corner = jnp.concatenate(block_inverse(tiles), axis=0)
+        pl.when(k == 0)(complete)
         row_id = lax.broadcasted_iota(jnp.int32, (size, B), 0)
         column = jnp.where(row_id >= (k + 1) * B, work[:, at], 0.0)
         unit = lax.broadcasted_iota(jnp.int32, (B, B), 0) == lax.broadcasted_iota(jnp.int32, (B, B), 1)
@@ -201,14 +203,26 @@
 
     for step in range(1, NEAR):
         end_copy(step, None).start()
-    for step in range(1, NEAR):
-        end_copy(step, 1).wait_recv()
-    for n, (i, j) in enumerate(blocks):
-        block = total[n * B : (n + 1) * B, :]
-        gram_ref[i * B : (i + 1) * B, j * B : (j + 1) * B] = block
-        if i != j:
-            gram_ref[j * B : (j + 1) * B, i * B : (i + 1) * B] = block.T
-    work[...] = gram_ref[...]
+
+    def share_in(index):
+        at = rows(index, share)
+        return pltpu.make_async_remote_copy(
+            src_ref=total.at[at], dst_ref=total.at[at], send_sem=end_s.at[1], recv_sem=end_r.at[index],
+            device_id=near_peer(1)[1], device_id_type=MESH)
+
+    def begin():
+        pl.when(rank != 0)(share_in(0).wait_recv)
+        work[:B, :B] = total[:B, :]
+
+    def complete():
+        for index in range(1, NEAR):
+            pl.when(rank != index)(share_in(index).wait_recv)
+        for n, (i, j) in enumerate(blocks):
+            block = total[n * B : (n + 1) * B, :]
+            gram_ref[i * B : (i + 1) * B, j * B : (j + 1) * B] = block
+            if i != j:
+                gram_ref[j * B : (j + 1) * B, i * B : (i + 1) * B] = block.T
+        work[...] = gram_ref[...]
 
     def target(index):
         return filtered_ref.at[index // 2, pl.ds(pl.multiple_of(lax.rem(index, 2) * 16, 8), ROWS // 2)]
@@ -235,7 +249,7 @@
             pl.when(jnp.logical_not(here))(lambda to_half=to_half: move(k, to_half).start())
             pl.when(here)(local.start)
 
-    factor_steps(work, rotate)
+    factor_steps(work, begin, complete, rotate)
     for step in range(1, NEAR):
         other, device = near_peer(step)
         pltpu.make_async_remote_copy(
@@ -286,8 +300,8 @@
 
 
 def whole_kernel(
-    factor, orb, pot, proj, info, gram_ref, filtered_ref,
-    e1, e2, second, shift_pot, nonlocal_plane, left, right, raw, notes, pot_all, corr_sum, corr, corr_in, weights,
+    factor, orb, pot, proj, coupling, planes, counts, gram_ref, filtered_ref,
+    e1, e2, second, shift_pot, nonlocal_plane, left, right, raw, notes, scratch_notes, pot_all, corr_sum, corr, corr_in, weights,
     give_cross, give_keep, got_cross, got1, got2, slab,
     local_s, x_s, x_r, own_s, fwd_s, halo_r, small_s, small_r, core_s, core_r, next_s, next_r, last_s, last_r,
     corr_s, corr_r, y2_s, y2_r, out_s, out_r, self_s,
@@ -329,12 +343,12 @@
     twin = pl.ds(pl.multiple_of((1 - core) * (PROJ // 2), 16), PROJ // 2)
     small = [
         send(pot, pot_all.at[pl.ds(4 * half, 4)], small_s.at[0], small_r.at[0], partner),
-        send(info, notes.at[1 + half], small_s.at[1], small_r.at[1], partner),
+        send(notes.at[1 + half], notes.at[1 + half], small_s.at[1], small_r.at[1], partner),
         send(raw.at[1 + half, share], raw.at[1 + half, share], small_s.at[2], small_r.at[2], partner),
     ]
     small_in = [
         send(pot, pot_all.at[pl.ds(4 * other, 4)], small_s.at[0], small_r.at[0], partner),
-        send(info, notes.at[1 + other], small_s.at[1], small_r.at[1], partner),
+        send(notes.at[1 + other], notes.at[1 + other], small_s.at[1], small_r.at[1], partner),
         send(raw.at[1 + other, share], raw.at[1 + other, share], small_s.at[2], small_r.at[2], partner),
     ]
     across = send(raw.at[1 + other, share], raw.at[1 + other, share], core_s, core_r, sibling)
@@ -367,7 +381,28 @@
         at = piece_rows(c)
         return send(give_keep.at[:, at], got1.at[side, :, at], own_s.at[c], halo_r.at[side, c], at_pair(1))
 
-    notes[1 + half] = info[...]
+    line = lax.broadcasted_iota(jnp.int32, (PROJ, WIDE), 0)
+    column = lax.broadcasted_iota(jnp.int32, (PROJ, WIDE), 1)
+    start, live = jnp.zeros_like(line), jnp.zeros_like(line)
+    for a in range(PROJ // MAXPROJ):
+        at_atom = (line >> 2) == a
+        start = jnp.where(at_atom, planes[a] - dom * 4, start)
+        live = jnp.where(at_atom, counts[a], live)
+        scratch_notes[a * MAXPROJ : (a + 1) * MAXPROJ, 0:MAXPROJ] = coupling[a]
+    same = (line >> 2) == (column >> 2)
+    spread_out = jnp.zeros((PROJ, WIDE), jnp.float32)
+    for j in range(MAXPROJ):
+        value = jnp.broadcast_to(scratch_notes[:, j : j + 1], (PROJ, WIDE))
+        spread_out = jnp.where(same & ((column & 3) == j), value, spread_out)
+    square = jnp.concatenate([spread_out, jnp.zeros((WIDE - PROJ, WIDE), jnp.float32)], axis=0)
+    symmetric = 0.5 * (spread_out + square.T[:PROJ])
+    symmetric = jnp.where(((line & 3) < live) & ((column & 3) < live), symmetric, 0.0)
+    wanted = jnp.full((PROJ, WIDE), -WIDE, jnp.int32)
+    for reach in range(REACH):
+        for k in range(SPAN):
+            wanted = jnp.where(column == FLAGS + reach * SPAN + k, reach - k, wanted)
+    flag_rows = jnp.where(wanted == start, 1.0, 0.0)
+    notes[1 + half] = jnp.where(column < FLAGS, symmetric, flag_rows)
     for a in range(PROJ // MAXPROJ):
         raw[1 + half, a * MAXPROJ : (a + 1) * MAXPROJ, :] = proj[a]
     pot_all[pl.ds(4 * half, 4)] = pot[...]
@@ -699,9 +734,10 @@
     finish_part(factor, gram_ref, filtered_ref, high_cells, low_cells, pack, *rest[:5], second, *rest[5:])
 
 
-def run(orbitals, potential, projectors, info, factor):
+def run(orbitals, potential, projectors, coupling, atom_plane, projector_count, factor):
     dma = pltpu.SemaphoreType.DMA
     f32, bf16 = jnp.float32, jnp.bfloat16
+    smem = pl.BlockSpec(memory_space=pltpu.SMEM)
     vmem, hbm = pl.BlockSpec(memory_space=pltpu.VMEM), pl.BlockSpec(memory_space=pl.ANY)
     block = (ROWS, DEPTH, WIDE)
     packed = len(tri_blocks(NORB)) * B
@@ -709,7 +745,7 @@
     return pl.pallas_call(
         functools.partial(whole_kernel, factor),
         out_shape=[jax.ShapeDtypeStruct((NORB, NORB), f32), jax.ShapeDtypeStruct((4,) + block, f32)],
-        in_specs=[hbm, vmem, vmem, vmem],
+        in_specs=[hbm, vmem, vmem, vmem, smem, smem],
         out_specs=[vmem, hbm],
         scratch_shapes=[
             pltpu.VMEM((12,) + block, f32),
@@ -721,6 +757,7 @@
             pltpu.VMEM((4, CELLS, 512), bf16),
             pltpu.VMEM((3, PROJ, SPAN * CELLS), f32),
             pltpu.VMEM((3, PROJ, 128), f32),
+            pltpu.VMEM((PROJ, MAXPROJ), f32),
             pltpu.VMEM((8, ROWS, DEPTH), f32),
             pltpu.VMEM((256, 2 * WIDE), f32),
             pltpu.VMEM((2, 3, PROJ, WIDE), f32),
@@ -749,29 +786,36 @@
             dma(()), dma((4, 2)), dma((NEAR,)),
         ],
         compiler_params=pltpu.CompilerParams(collective_id=2, has_side_effects=True, vmem_limit_bytes=62 * 2**20),
-    )(orbitals, potential, projectors, info)
+    )(orbitals, potential, projectors, coupling, atom_plane, projector_count)
+
+
+def settle_kernel(gram, filtered, gram_out, filtered_out, sems):
+    copies = [pltpu.make_async_copy(filtered.at[p], filtered_out.at[p], sems.at[p]) for p in range(4)]
+    copies.append(pltpu.make_async_copy(gram, gram_out, sems.at[4]))
+    for copy in copies:
+        copy.start()
+    for copy in copies:
+        copy.wait()
+
+
+def settle(gram, filtered):
+    hbm = pl.BlockSpec(memory_space=pl.ANY)
+    return pl.pallas_call(
+        settle_kernel,
+        out_shape=[jax.ShapeDtypeStruct(x.shape, x.dtype) for x in (gram, filtered)],
+        in_specs=[hbm, hbm],
+        out_specs=[hbm, hbm],
+        scratch_shapes=[pltpu.SemaphoreType.DMA((5,))],
+        compiler_params=pltpu.CompilerParams(vmem_limit_bytes=8 * 2**20),
+    )(gram, filtered)
 
 
 def shards(orbitals, potential, projectors, coupling, atom_plane, projector_count):
-    planes, side_y, side_z, local_orbs = orbitals.shape
-    atoms = projectors.shape[0]
-    first_plane = atom_plane - lax.axis_index("dom") * planes
-    reach_ids = jnp.arange(REACH, dtype=jnp.int32)
-    span_ids = jnp.arange(SPAN, dtype=jnp.int32)
-    flags = (
-        reach_ids[None, :, None] == first_plane[:, None, None] + span_ids[None, None, :]
-    ).astype(jnp.float32).reshape(atoms, 1, REACH * SPAN)
-    flags = jnp.broadcast_to(flags, (atoms, MAXPROJ, REACH * SPAN)).reshape(PROJ, REACH * SPAN)
-    slots = jnp.arange(MAXPROJ, dtype=jnp.int32)
-    live_mask = (slots[None, :] < projector_count[:, None]).astype(jnp.float32)
-    sym_coupling = 0.5 * (coupling + jnp.transpose(coupling, (0, 2, 1)))
-    sym_coupling = sym_coupling * live_mask[:, :, None] * live_mask[:, None, :]
-    same_atom = jnp.eye(atoms, dtype=jnp.float32)
-    blocks = (sym_coupling[:, :, None, :] * same_atom[:, None, :, None]).reshape(PROJ, PROJ)
-    info = jnp.concatenate(
-        [blocks, flags, jnp.zeros((PROJ, 128 - PROJ - REACH * SPAN), jnp.float32)], axis=1)
+    planes, side_y, side_z, _ = orbitals.shape
     total_cells = planes * side_y * side_z * lax.axis_size("dom")
-    gram, filtered = run(orbitals, potential, projectors, info, 1.0 / total_cells)
+    gram, filtered = run(
+        orbitals, potential, projectors, coupling, atom_plane, projector_count, 1.0 / total_cells)
+    gram, filtered = settle(gram, filtered)
     return (filtered, gram)
 
 

time: 220 us -> 215 us (0.977)
  other arithmetic: 3.6 us -> 0 us
    pallas_call x1, Pallas kernels: 209 us -> 205 us  [run(): pl.pallas_call(functools.partial(whole_kernel, factor), out_shape=[jax.Sh...]
    unnamed x4 -> x5, local copies, waits for them, and re-layouts: 4.93 us -> 4.5 us
where the time goes in v6:
time: 215 us; the launch traced here: 212 us
  Pallas kernels  207 us (96%)
  local copies, waits for them, and re-layouts  4.5 us (2%)
    pallas_call x1, Pallas kernels, run(): pl.pallas_call(functools.partial(whole_kernel, factor), out_shape=[jax.Sh...  205 us
    unnamed x5, local copies, waits for them, and re-layouts  4.5 us

profile of v6, /device:TPU:0, one launch (start us, length us, event | category | flops | bytes accessed | tf_op | source)
XLA Modules:
  0.0 212.0 jit_solution(13374038559227716849)
XLA Ops:
  0.6 1.4 copy.8.coupling
  2.0 204.7 %shard_map.77 = (f32[512,512]{1,0:T(8,128)}, f32[4,32,48,128]{3,2,1,0:T(8,128)}) custom-call(f32[4,32,48,128]{3,2,1,0:T(8,128)} %orb.1, f32[4,32,48]{2,1,0:T(8,128)} %pot.1, f32[8,4,4608]{2,1,0:T(4,128)} %proj.1, f32[8,4,4]{2,1,0:T(4,128)} %copy.8.coupling, s32[8]{0:T(128)} %planes.1, s32[8]{0:T(128)} %counts.1), custom_call_target="tpu_custom_call" | custom-call | tf_op jit(solution)/shard_map/pallas_call | solution.py:745
  206.7 0.0 copy-start
  206.7 1.9 copy-done
  208.6 0.0 copy-start.1
  208.6 1.2 copy-done.1
  209.8 2.0 shard_map.78
Async XLA Ops:
  206.7 1.9 copy-start
  208.6 1.2 copy-start.1

commit v7 on v6

--- a/solution.py
+++ b/solution.py
@@ -534,9 +534,9 @@
             parts += [high_part, high_part, low_part, zero]
         weights[...] = jnp.concatenate(parts, axis=0)
 
-    def open_strip(field, got, strip):
+    def open_rows(field, got, base, count):
         def one(n, carry):
-            r = strip * STRIP + n
+            r = base + n
             for j in range(2):
                 near, far = field[4 + j, r], field[6 + j, r]
                 up, down = got[0, j, r], got[1, j, r]
@@ -546,17 +546,17 @@
                 field[10 + j, r] = jnp.where(lower, swap(far), down)
             return carry
 
-        lax.fori_loop(0, STRIP, one, 0)
-
-    def apply(field, strip, scale, write):
+        lax.fori_loop(0, count, one, 0)
+
+    def apply(field, base, count, scale, write):
         def plane(p, carry):
             product = lax.dot_general(
-                right[p, pl.ds(pl.multiple_of(strip * AREA, AREA), AREA), :], weights[...],
+                right[p, base * DEPTH : (base + count) * DEPTH, :], weights[...],
                 (((1,), (0,)), ((), ())), preferred_element_type=jnp.float32)
-            nonlocal_plane[...] = product.reshape(STRIP, DEPTH, WIDE)
+            nonlocal_plane[:count] = product.reshape(count, DEPTH, WIDE)
 
             def row(n, inner):
-                r = strip * STRIP + n
+                r = base + n
                 centre = field[p + 4, r]
                 total = centre * shift_pot[p, r] + nonlocal_plane[n]
                 for k in range(1, 5):
@@ -567,7 +567,7 @@
                 write(p, r, total * scale)
                 return inner
 
-            lax.fori_loop(0, STRIP, row, 0)
+            lax.fori_loop(0, count, row, 0)
             return carry
 
         lax.fori_loop(0, 4, plane, 0)
@@ -576,7 +576,7 @@
         for side in range(2):
             for n in range(STRIP // PIECE):
                 halo_in(side, strip * (STRIP // PIECE) + n).wait_recv()
-        open_strip(e1, got1, strip)
+        open_rows(e1, got1, strip * STRIP, STRIP)
 
     spread_rows(0)
     across_in.wait_recv()
@@ -631,7 +631,7 @@
         return send(give_keep.at[:, at], got2.at[1, :, at], y2_s.at[1, c], y2_r.at[1, c], at_pair(-1))
 
     def first_strip(strip):
-        apply(e1, strip, 1.0 / 6.0, write_first)
+        apply(e1, strip * STRIP, STRIP, 1.0 / 6.0, write_first)
 
         def pack(n, inner):
             r = strip * STRIP + n
@@ -657,32 +657,31 @@
         second[p, r] = value - e1[p + 4, r]
 
     def give(index, part):
-        src = second.at[index // 2, pl.ds(lax.rem(index, 2) * 16 + part * STRIP, STRIP)]
-        return send(src, slab.at[rank, pl.ds(part * STRIP, STRIP)], out_s.at[index, part], out_r.at[rank, part],
+        src = second.at[index // 2, pl.ds(lax.rem(index, 2) * 16 + part * PIECE, PIECE)]
+        return send(src, slab.at[rank, pl.ds(part * PIECE, PIECE)], out_s.at[index, part], out_r.at[rank, part],
                     member(index))
 
     def own_part(part):
-        src = second.at[rank // 2, pl.ds(lax.rem(rank, 2) * 16 + part * STRIP, STRIP)]
-        return pltpu.make_async_copy(src, slab.at[rank, pl.ds(part * STRIP, STRIP)], self_s.at[part])
-
-    def second_strip(strip):
-        for c in range(2 * strip, 2 * strip + 2):
-            for copy in (up2(c), down2(c)):
-                copy.wait_recv()
-                copy.wait_send()
-            if c + WINDOW < PIECES:
-                up2(c + WINDOW).start()
-                down2(c + WINDOW).start()
-        open_strip(e2, got2, strip)
-        apply(e2, strip, 1.0 / 3.0, write_second)
-        part = strip % 2
+        src = second.at[rank // 2, pl.ds(lax.rem(rank, 2) * 16 + part * PIECE, PIECE)]
+        return pltpu.make_async_copy(src, slab.at[rank, pl.ds(part * PIECE, PIECE)], self_s.at[part])
+
+    def second_piece(c):
+        for copy in (up2(c), down2(c)):
+            copy.wait_recv()
+            copy.wait_send()
+        if c + WINDOW < PIECES:
+            up2(c + WINDOW).start()
+            down2(c + WINDOW).start()
+        open_rows(e2, got2, c * PIECE, PIECE)
+        apply(e2, c * PIECE, PIECE, 1.0 / 3.0, write_second)
+        row_half, part = c // 4, c % 4
         for n in range(4):
-            index = 2 * lax.rem(n + rank // 2 + 2, 4) + strip // 2
+            index = 2 * lax.rem(n + rank // 2 + 2, 4) + row_half
             pl.when(index != rank)(lambda index=index: give(index, part).start())
-        pl.when(lax.rem(rank, 2) == strip // 2)(own_part(part).start)
-
-    for strip in range(STRIPS):
-        second_strip(strip)
+        pl.when(lax.rem(rank, 2) == row_half)(own_part(part).start)
+
+    for c in range(PIECES):
+        second_piece(c)
 
     blocks = tri_blocks(NORB)
     pack[...] = jnp.zeros_like(pack)
@@ -717,19 +716,20 @@
 
         lax.fori_loop(0, 2, chunk, 0)
 
-    for part in range(2):
-        for n in range(1, GROUP):
-            index = lax.rem(rank + n, GROUP)
-            send(second.at[0, pl.ds(0, STRIP)], slab.at[index, pl.ds(part * STRIP, STRIP)], out_s.at[index, part],
-                 out_r.at[index, part], member(index)).wait_recv()
-        own_part(part).wait()
-        lax.fori_loop(part * STRIP, (part + 1) * STRIP, repack, 0)
-        add_gram(part)
+    for section in range(2):
+        for part in (2 * section, 2 * section + 1):
+            for n in range(1, GROUP):
+                index = lax.rem(rank + n, GROUP)
+                send(second.at[0, pl.ds(0, PIECE)], slab.at[index, pl.ds(part * PIECE, PIECE)],
+                     out_s.at[index, part], out_r.at[index, part], member(index)).wait_recv()
+            own_part(part).wait()
+            lax.fori_loop(part * PIECE, (part + 1) * PIECE, repack, 0)
+        add_gram(section)
 
     for copy in small + [across, last] + onward + copies1 + copies2:
         copy.wait_send()
     for n in range(1, GROUP):
-        for part in range(2):
+        for part in range(4):
             give(lax.rem(rank + n, GROUP), part).wait_send()
     finish_part(factor, gram_ref, filtered_ref, high_cells, low_cells, pack, *rest[:5], second, *rest[5:])
 
@@ -772,7 +772,7 @@
             dma((4,)), dma((PIECES,)), dma((PIECES,)), dma((PIECES,)), dma((PIECES,)), dma((2, PIECES)),
             dma((3,)), dma((3,)), dma(()), dma(()), dma((2,)), dma((2,)), dma(()), dma(()),
             dma((2, 2)), dma((2, 2)), dma((2, PIECES)), dma((2, PIECES)),
-            dma((GROUP, 2)), dma((GROUP, 2)), dma((2,)),
+            dma((GROUP, 4)), dma((GROUP, 4)), dma((4,)),
             pltpu.VMEM((CELLS, NORB), bf16),
             pltpu.VMEM((CELLS, NORB), bf16),
             pltpu.VMEM((packed, B), f32),

time: 215 us -> 214 us (level)
  no operation moved by 1% of the time
where the time goes in v7:
time: 214 us; the launch traced here: 211 us
  Pallas kernels  205 us (96%)
  local copies, waits for them, and re-layouts  4.5 us (2%)
    pallas_call x1, Pallas kernels, run(): pl.pallas_call(functools.partial(whole_kernel, factor), out_shape=[jax.Sh...  203 us
    unnamed x5, local copies, waits for them, and re-layouts  4.5 us

profile of v7, /device:TPU:0, one launch (start us, length us, event | category | flops | bytes accessed | tf_op | source)
XLA Modules:
  0.0 210.6 jit_solution(9475047136494097421)
XLA Ops:
  0.6 1.4 copy.8.coupling
  2.0 203.3 %shard_map.77 = (f32[512,512]{1,0:T(8,128)}, f32[4,32,48,128]{3,2,1,0:T(8,128)}) custom-call(f32[4,32,48,128]{3,2,1,0:T(8,128)} %orb.1, f32[4,32,48]{2,1,0:T(8,128)} %pot.1, f32[8,4,4608]{2,1,0:T(4,128)} %proj.1, f32[8,4,4]{2,1,0:T(4,128)} %copy.8.coupling, s32[8]{0:T(128)} %planes.1, s32[8]{0:T(128)} %counts.1), custom_call_target="tpu_custom_call" | custom-call | tf_op jit(solution)/shard_map/pallas_call | solution.py:745
  205.3 0.0 copy-start
  205.3 1.9 copy-done
  207.2 0.0 copy-start.1
  207.2 1.2 copy-done.1
  208.4 2.0 shard_map.78
Async XLA Ops:
  205.3 1.9 copy-start
  207.2 1.2 copy-start.1

commit v8 on v7

--- a/solution.py
+++ b/solution.py
@@ -83,8 +83,16 @@
         unit = lax.broadcasted_iota(jnp.int32, (B, B), 0) == lax.broadcasted_iota(jnp.int32, (B, B), 1)
         work[at, at] = jnp.where(unit, 1.0, 0.0)
         scaled = dot_f32(corner, work[at, :], ((1,), (0,)))
-        row_at = lax.broadcasted_iota(jnp.int32, (B, size), 0) + k * B
-        done(k, jnp.where(lax.broadcasted_iota(jnp.int32, (B, size), 1) <= row_at, scaled, 0.0))
+        work[at, :] = scaled
+
+        def hand_on(n, inner):
+            block = k - n
+            rows = work[pl.ds(pl.multiple_of(block * B, B), B), :]
+            row_at = lax.broadcasted_iota(jnp.int32, (B, size), 0) + block * B
+            done(block, jnp.where(lax.broadcasted_iota(jnp.int32, (B, size), 1) <= row_at, rows, 0.0))
+            return inner
+
+        lax.fori_loop(0, jnp.where(k == 1, 0, jnp.where(k == 2, 2, 1)), hand_on, 0)
         below = dot_f32(column, corner, ((1,), (1,)))
         block = work[:, at]
         work[:, at] = jnp.where(row_id >= (k + 1) * B, 0.0, block)

time: 214 us -> 210 us (0.981)
  no operation moved by 1% of the time
where the time goes in v8:
time: 210 us; the launch traced here: 209 us
  Pallas kernels  203 us (97%)
  local copies, waits for them, and re-layouts  4.5 us (2%)
    pallas_call x1, Pallas kernels, run(): pl.pallas_call(functools.partial(whole_kernel, factor), out_shape=[jax.Sh...  201 us
    unnamed x5, local copies, waits for them, and re-layouts  4.5 us

profile of v8, /device:TPU:0, one launch (start us, length us, event | category | flops | bytes accessed | tf_op | source)
XLA Modules:
  0.0 208.7 jit_solution(14124677257281800529)
XLA Ops:
  0.6 1.4 copy.8.coupling
  2.0 201.4 %shard_map.77 = (f32[512,512]{1,0:T(8,128)}, f32[4,32,48,128]{3,2,1,0:T(8,128)}) custom-call(f32[4,32,48,128]{3,2,1,0:T(8,128)} %orb.1, f32[4,32,48]{2,1,0:T(8,128)} %pot.1, f32[8,4,4608]{2,1,0:T(4,128)} %proj.1, f32[8,4,4]{2,1,0:T(4,128)} %copy.8.coupling, s32[8]{0:T(128)} %planes.1, s32[8]{0:T(128)} %counts.1), custom_call_target="tpu_custom_call" | custom-call | tf_op jit(solution)/shard_map/pallas_call | solution.py:753
  203.4 0.0 copy-start
  203.4 1.9 copy-done
  205.3 0.0 copy-start.1
  205.3 1.2 copy-done.1
  206.5 2.0 shard_map.78
Async XLA Ops:
  203.4 1.9 copy-start
  205.3 1.2 copy-start.1

commit v9 on v8

--- a/solution.py
+++ b/solution.py
@@ -430,11 +430,11 @@
         cross(c).start()
         keep(c).start()
 
-    lax.fori_loop(0, WINDOW, pack_piece, 0)
     pl.semaphore_wait(barrier, GROUP + FAR - 2)
     for copy in small:
         copy.start()
     for c in range(WINDOW):
+        pack_piece(c, 0)
         start_piece(c)
     lax.fori_loop(WINDOW, PIECES, pack_piece, 0)
 

time: 210 us -> 210 us (level)
  no operation moved by 1% of the time
where the time goes in v9:
time: 210 us; the launch traced here: 208 us
  Pallas kernels  203 us (97%)
  local copies, waits for them, and re-layouts  4.5 us (2%)
    pallas_call x1, Pallas kernels, run(): pl.pallas_call(functools.partial(whole_kernel, factor), out_shape=[jax.Sh...  201 us
    unnamed x5, local copies, waits for them, and re-layouts  4.5 us

profile of v9, /device:TPU:0, one launch (start us, length us, event | category | flops | bytes accessed | tf_op | source)
XLA Modules:
  0.0 208.3 jit_solution(17454120337210531694)
XLA Ops:
  0.6 1.4 copy.8.coupling
  2.0 200.9 %shard_map.77 = (f32[512,512]{1,0:T(8,128)}, f32[4,32,48,128]{3,2,1,0:T(8,128)}) custom-call(f32[4,32,48,128]{3,2,1,0:T(8,128)} %orb.1, f32[4,32,48]{2,1,0:T(8,128)} %pot.1, f32[8,4,4608]{2,1,0:T(4,128)} %proj.1, f32[8,4,4]{2,1,0:T(4,128)} %copy.8.coupling, s32[8]{0:T(128)} %planes.1, s32[8]{0:T(128)} %counts.1), custom_call_target="tpu_custom_call" | custom-call | tf_op jit(solution)/shard_map/pallas_call | solution.py:753
  202.9 0.0 copy-start
  203.0 1.9 copy-done
  204.8 0.0 copy-start.1
  204.8 1.2 copy-done.1
  206.1 2.0 shard_map.78
Async XLA Ops:
  202.9 1.9 copy-start
  204.8 1.2 copy-start.1
